TPU v7x, 32 devices: a whole 2x2x4 slice. The times are simulated.
32 devices in a mesh: dp: 8 (over y, x, core), blk: 4 (over z).
Axes of the slice: x: 2, y: 2, z: 4, core: 2. Of those that a mesh axis runs over, the one named last changes fastest.
Arguments:
- clips: bfloat16 [64, 8, 8, 8, 528], P('dp', 'blk'), may hold values from -19 to 19
- cotangent: bfloat16 [64, 4, 4, 4, 832], P('dp', 'blk'), may hold values from -19 to 19
- entry_4f: bfloat16 [2, 236544], P(None, 'blk'), may hold values from -0.25 to 0.25
- wide_4f: bfloat16 [2, 1382400], P(None, 'blk'), may hold values from -0.09375 to 0.09375
- narrow_4f: bfloat16 [2, 110592], P(None, 'blk'), may hold values from -0.21875 to 0.21875
- poolproj_4f: bfloat16 [2, 67584], P(None, 'blk'), may hold values from -0.25 to 0.25
- gain_4f: bfloat16 [2, 1024], P(None, 'blk'), may hold values from 0.099609375 to 1.8984375
- shift_4f: bfloat16 [2, 1024], P(None, 'blk'), may hold values from -2.5 to 2.5
- entry_5b: bfloat16 [2, 372736], P(None, 'blk'), may hold values from -0.21875 to 0.21875
- wide_5b: bfloat16 [2, 1382400], P(None, 'blk'), may hold values from -0.09375 to 0.09375
- narrow_5b: bfloat16 [2, 110592], P(None, 'blk'), may hold values from -0.21875 to 0.21875
- poolproj_5b: bfloat16 [2, 106496], P(None, 'blk'), may hold values from -0.21875 to 0.21875
- gain_5b: bfloat16 [2, 1024], P(None, 'blk'), may hold values from 0.099609375 to 1.8984375
- shift_5b: bfloat16 [2, 1024], P(None, 'blk'), may hold values from -2.5 to 2.5
Outputs:
- features: float32 [64, 4, 4, 4, 832], P('dp', 'blk')
- clips_grad: float32 [64, 8, 8, 8, 528], P('dp', 'blk')
- entry_4f_grad: float32 [2, 236544], P(None, 'blk')
- wide_4f_grad: float32 [2, 1382400], P(None, 'blk')
- narrow_4f_grad: float32 [2, 110592], P(None, 'blk')
- poolproj_4f_grad: float32 [2, 67584], P(None, 'blk')
- gain_4f_grad: float32 [2, 1024], P(None, 'blk')
- shift_4f_grad: float32 [2, 1024], P(None, 'blk')
- entry_5b_grad: float32 [2, 372736], P(None, 'blk')
- wide_5b_grad: float32 [2, 1382400], P(None, 'blk')
- narrow_5b_grad: float32 [2, 110592], P(None, 'blk')
- poolproj_5b_grad: float32 [2, 106496], P(None, 'blk')
- gain_5b_grad: float32 [2, 1024], P(None, 'blk')
- shift_5b_grad: float32 [2, 1024], P(None, 'blk')
All inputs are finite; a program needn't handle non-finite values.
Results may differ from a plain program's by a relative error of at most 0.022.
Values may be sent and summed in bfloat16 or wider, within the bound.
No kernel may reach another device: no remote copies, remote signals or barrier semaphores. Data moves between devices by JAX's collectives and lax.ppermute only.
A program may use at most 256 MiB of HBM per device.

v0:
```python
import jax
import jax.numpy as jnp
from jax import lax
from jax.sharding import PartitionSpec as P

B0 = 256
B1R = 160
B1 = 320
B2R = 32
B2 = 128
BP = 128


EPS = 1e-05
SPATIAL = ((0, 0), (0, 0), (1, 1), (1, 1), (0, 0))


def padded_2(block, sides, width):
    for axis, dim in sides:
        count = lax.axis_size(axis)
        forward = [(i, i + 1) for i in range(count - 1)]
        backward = [(target, source) for source, target in forward]
        low = lax.ppermute(
            lax.slice_in_dim(block, block.shape[dim] - width, None, axis=dim), axis, forward
        )
        high = lax.ppermute(lax.slice_in_dim(block, 0, width, axis=dim), axis, backward)
        block = jnp.concatenate([low, block, high], axis=dim)
    return block


def tap_region(tap_index, frames, height, breadth):
    depth_off = tap_index // 9
    row_off = tap_index // 3 % 3
    col_off = tap_index % 3
    return (
        slice(None),
        slice(depth_off, depth_off + frames),
        slice(row_off, row_off + height),
        slice(col_off, col_off + breadth),
    )


def window(padded, tap_index, frames, height, breadth):
    return padded[tap_region(tap_index, frames, height, breadth)]


def conv_taps(padded, kernel, frames, height, breadth):
    summed = jnp.einsum(
        "nfhwc,cd->nfhwd",
        window(padded, 0, frames, height, breadth),
        kernel[0],
        preferred_element_type=jnp.float32,
    )
    for tap_index in range(1, 27):
        summed = summed + jnp.einsum(
            "nfhwc,cd->nfhwd",
            window(padded, tap_index, frames, height, breadth),
            kernel[tap_index],
            preferred_element_type=jnp.float32,
        )
    return summed


def conv_back(grad, kernel, frames, height, breadth):
    padded_grad = jnp.pad(grad, ((0, 0), (2, 2), (1, 1), (1, 1), (0, 0)))
    flipped = jnp.swapaxes(kernel, 1, 2)[::-1]
    return conv_taps(padded_grad, flipped, frames + 2, height, breadth)


def pool_sum(padded, frames, height, breadth):
    values = padded.astype(jnp.float32)
    values = values[:, 0:frames] + values[:, 1 : frames + 1] + values[:, 2 : frames + 2]
    values = values[:, :, 0:height] + values[:, :, 1 : height + 1] + values[:, :, 2 : height + 2]
    values = (
        values[:, :, :, 0:breadth]
        + values[:, :, :, 1 : breadth + 1]
        + values[:, :, :, 2 : breadth + 2]
    )
    return values / 27.0


def pool_spread(values):
    frames, height, breadth = (values.shape[1], values.shape[2], values.shape[3])
    spread = jnp.pad(values, ((0, 0), (2, 2), (0, 0), (0, 0), (0, 0)))
    spread = spread[:, 0 : frames + 2] + spread[:, 1 : frames + 3] + spread[:, 2 : frames + 4]
    spread = jnp.pad(spread, ((0, 0), (0, 0), (1, 1), (0, 0), (0, 0)))
    spread = spread[:, :, 0:height] + spread[:, :, 1 : height + 1] + spread[:, :, 2 : height + 2]
    spread = jnp.pad(spread, ((0, 0), (0, 0), (0, 0), (1, 1), (0, 0)))
    return (
        spread[:, :, :, 0:breadth]
        + spread[:, :, :, 1 : breadth + 1]
        + spread[:, :, :, 2 : breadth + 2]
    )


def local_pair(values, other):
    return (jnp.sum(values, axis=(0, 1, 2, 3)), jnp.sum(values * other, axis=(0, 1, 2, 3)))


def place_row(vector, stream):
    rows_index = jnp.arange(2).reshape(2, 1)
    return jnp.where(rows_index == stream, vector[None, :], 0.0)


def pick_row(matrix, stream):
    return lax.dynamic_index_in_dim(matrix, stream, 0, keepdims=False)


def share_sums(couples, stream):
    shared = []
    for couple in couples:
        shared.append(
            lax.psum((place_row(couple[0], stream), place_row(couple[1], stream)), ("dp", "blk"))
        )
    return shared


def normalize(values, sums_pair, gain, shift, voxels, stream):
    centre = pick_row(sums_pair[0], stream) / voxels
    spread = lax.rsqrt(pick_row(sums_pair[1], stream) / voxels - centre * centre + EPS)
    scaled = (values - centre) * spread
    return (scaled * gain + shift, scaled, spread)


def silu_slope(values):
    sigmoid = jax.nn.sigmoid(values)
    return sigmoid * (1.0 + values * (1.0 - sigmoid))


def norm_back(slope_grad, scaled, spread, gain, sums_pair, voxels, stream):
    mean_grad = pick_row(sums_pair[0], stream) / voxels
    mean_cross = pick_row(sums_pair[1], stream) / voxels
    return (gain * spread * (slope_grad - mean_grad - scaled * mean_cross)).astype(jnp.bfloat16)


def layer_spans(weights):
    reduced = weights[0].shape[1]
    wide_end = reduced + weights[1].shape[2]
    narrow_end = wide_end + weights[2].shape[2]
    return [
        (0, reduced),
        (reduced, wide_end),
        (wide_end, narrow_end),
        (narrow_end, narrow_end + weights[3].shape[1]),
    ]


def frame_rims(joined):
    return padded_2(joined, (("blk", 1),), 1)


def forward_layer(inputs_low, weights, stream, voxels):
    entry, wide, narrow, poolproj = (weights[0], weights[1], weights[2], weights[3])
    gain = weights[4].astype(jnp.float32)
    shift = weights[5].astype(jnp.float32)
    spans = layer_spans(weights)
    channels = inputs_low.shape[4]
    frames, height, breadth = (inputs_low.shape[1], inputs_low.shape[2], inputs_low.shape[3])
    inner_wide = wide.shape[1]
    direct = entry.shape[1] - inner_wide - narrow.shape[1]
    reduced = spans[0][1]
    front = jnp.einsum("nfhwc,cd->nfhwd", inputs_low, entry, preferred_element_type=jnp.float32)
    front_sums = share_sums([local_pair(front, front)], stream)[0]
    front_norm = normalize(front, front_sums, gain[:reduced], shift[:reduced], voxels, stream)
    front_act = jax.nn.silu(front_norm[0])
    joined = jnp.concatenate([inputs_low, front_act[..., direct:].astype(jnp.bfloat16)], axis=4)
    rimmed = frame_rims(joined)
    padded = jnp.pad(rimmed, SPATIAL)
    pooled = pool_sum(padded[..., :channels], frames, height, breadth).astype(jnp.bfloat16)
    wide_out = conv_taps(
        padded[..., channels : channels + inner_wide], wide, frames, height, breadth
    )
    narrow_out = conv_taps(padded[..., channels + inner_wide :], narrow, frames, height, breadth)
    pool_out = jnp.einsum("nfhwc,cd->nfhwd", pooled, poolproj, preferred_element_type=jnp.float32)
    branches = [wide_out, narrow_out, pool_out]
    branch_sums = share_sums([local_pair(branch, branch) for branch in branches], stream)
    pieces = [front_act[..., :direct]]
    for number in range(3):
        low_edge, high_edge = spans[number + 1]
        normed = normalize(
            branches[number],
            branch_sums[number],
            gain[low_edge:high_edge],
            shift[low_edge:high_edge],
            voxels,
            stream,
        )
        pieces.append(jax.nn.silu(normed[0]))
    return (
        jnp.concatenate(pieces, axis=4),
        (front, front_sums, padded, pooled, branches, branch_sums),
    )


def backward_layer(grad_out, inputs_low, weights, kept, stream, voxels):
    entry, wide, narrow, poolproj = (weights[0], weights[1], weights[2], weights[3])
    gain = weights[4].astype(jnp.float32)
    spans = layer_spans(weights)
    front, front_sums, padded, pooled, branches, branch_sums = kept
    channels = inputs_low.shape[4]
    frames, height, breadth = (inputs_low.shape[1], inputs_low.shape[2], inputs_low.shape[3])
    inner_wide = wide.shape[1]
    direct = entry.shape[1] - inner_wide - narrow.shape[1]
    reduced = spans[0][1]
    shift = weights[5].astype(jnp.float32)
    slopes = []
    couples = []
    column = direct
    for number in range(3):
        low_edge, high_edge = spans[number + 1]
        normed = normalize(
            branches[number],
            branch_sums[number],
            gain[low_edge:high_edge],
            shift[low_edge:high_edge],
            voxels,
            stream,
        )
        extent = high_edge - low_edge
        slope_grad = grad_out[..., column : column + extent] * silu_slope(normed[0])
        column = column + extent
        slopes.append((slope_grad, normed[1], normed[2]))
        couples.append(local_pair(slope_grad, normed[1]))
    branch_back = share_sums(couples, stream)
    rounded = []
    for number in range(3):
        low_edge, high_edge = spans[number + 1]
        rounded.append(
            norm_back(
                slopes[number][0],
                slopes[number][1],
                slopes[number][2],
                gain[low_edge:high_edge],
                branch_back[number],
                voxels,
                stream,
            )
        )
    wide_grad, narrow_grad, pool_grad = (rounded[0], rounded[1], rounded[2])
    pool_back = (
        jnp.einsum("nfhwd,cd->nfhwc", pool_grad, poolproj, preferred_element_type=jnp.float32)
        / 27.0
    )
    grad_pool = pool_spread(pool_back)
    grad_wide = conv_back(wide_grad, wide, frames, height, breadth)
    grad_narrow = conv_back(narrow_grad, narrow, frames, height, breadth)
    wide_pad = padded[..., channels : channels + inner_wide]
    narrow_pad = padded[..., channels + inner_wide :]
    wide_taps = []
    narrow_taps = []
    for tap_index in range(27):
        wide_taps.append(
            jnp.einsum(
                "nfhwc,nfhwd->cd",
                window(wide_pad, tap_index, frames, height, breadth),
                wide_grad,
                preferred_element_type=jnp.float32,
            )
        )
        narrow_taps.append(
            jnp.einsum(
                "nfhwc,nfhwd->cd",
                window(narrow_pad, tap_index, frames, height, breadth),
                narrow_grad,
                preferred_element_type=jnp.float32,
            )
        )
    grad_pad = jnp.concatenate([grad_pool, grad_wide, grad_narrow], axis=4)
    rim_pair = jnp.concatenate([grad_pad[:, :1], grad_pad[:, -1:]], axis=1)
    arrived = padded_2(rim_pair.astype(jnp.bfloat16), (("blk", 1),), 1).astype(rim_pair.dtype)
    interior = grad_pad[:, 1:-1]
    interior = interior.at[:, 0].add(arrived[:, 0])
    interior = interior.at[:, frames - 1].add(arrived[:, 3])
    front_norm = normalize(front, front_sums, gain[:reduced], shift[:reduced], voxels, stream)
    front_act_grad = jnp.concatenate([grad_out[..., :direct], interior[..., channels:]], axis=4)
    front_slope = front_act_grad * silu_slope(front_norm[0])
    front_back = share_sums([local_pair(front_slope, front_norm[1])], stream)[0]
    front_grad = norm_back(
        front_slope, front_norm[1], front_norm[2], gain[:reduced], front_back, voxels, stream
    )
    grad_inputs = (
        jnp.einsum("nfhwd,cd->nfhwc", front_grad, entry, preferred_element_type=jnp.float32)
        + interior[..., :channels]
    )
    entry_grad = jnp.einsum(
        "nfhwc,nfhwd->dc", inputs_low, front_grad, preferred_element_type=jnp.float32
    )
    pool_weight_grad = jnp.einsum(
        "nfhwc,nfhwd->dc", pooled, pool_grad, preferred_element_type=jnp.float32
    )
    local_grads = (
        entry_grad.reshape(-1),
        jnp.stack(wide_taps).transpose(2, 0, 1).reshape(-1),
        jnp.stack(narrow_taps).transpose(2, 0, 1).reshape(-1),
        pool_weight_grad.reshape(-1),
    )
    gain_rows = jnp.concatenate([front_back[1]] + [couple[1] for couple in branch_back], axis=1)
    shift_rows = jnp.concatenate([front_back[0]] + [couple[0] for couple in branch_back], axis=1)
    return (grad_inputs, local_grads, (gain_rows, shift_rows))


def own_slices(params, stream):
    return tuple((lax.dynamic_index_in_dim(tensor, stream, 0, keepdims=False) for tensor in params))


def unflatten(gathered):
    reduced = B0 + B1R + B2R
    entry = gathered[0].reshape(reduced, -1).T
    wide = gathered[1].reshape(B1, 27, B1R).transpose(1, 2, 0)
    narrow = gathered[2].reshape(B2, 27, B2R).transpose(1, 2, 0)
    poolproj = gathered[3].reshape(BP, -1).T
    return (entry, wide, narrow, poolproj, gathered[4], gathered[5])


def fetch_weights(params, stream):
    own_shards = own_slices(params, stream)
    gathered = (
        lax.all_gather(own_shards[0], "blk", axis=0, tiled=True),
        lax.all_gather(own_shards[1], "blk", axis=0, tiled=True),
        lax.all_gather(own_shards[2], "blk", axis=0, tiled=True),
        lax.all_gather(own_shards[3], "blk", axis=0, tiled=True),
        lax.all_gather(own_shards[4], "blk", axis=0, tiled=True),
        lax.all_gather(own_shards[5], "blk", axis=0, tiled=True),
    )
    return unflatten(gathered)


def refetch_weights(params, stream):
    own_shards = own_slices(params, stream)
    gathered = (
        lax.all_gather(own_shards[0], "blk", axis=0, tiled=True),
        lax.all_gather(own_shards[1], "blk", axis=0, tiled=True),
        lax.all_gather(own_shards[2], "blk", axis=0, tiled=True),
        lax.all_gather(own_shards[3], "blk", axis=0, tiled=True),
        lax.all_gather(own_shards[4], "blk", axis=0, tiled=True),
        lax.all_gather(own_shards[5], "blk", axis=0, tiled=True),
    )
    return unflatten(gathered)


def reduce_grads(local_grads, stream):
    shards = (
        lax.psum_scatter(
            local_grads[0].astype(jnp.bfloat16), "blk", scatter_dimension=0, tiled=True
        ).astype(jnp.float32),
        lax.psum_scatter(
            local_grads[1].astype(jnp.bfloat16), "blk", scatter_dimension=0, tiled=True
        ).astype(jnp.float32),
        lax.psum_scatter(
            local_grads[2].astype(jnp.bfloat16), "blk", scatter_dimension=0, tiled=True
        ).astype(jnp.float32),
        lax.psum_scatter(
            local_grads[3].astype(jnp.bfloat16), "blk", scatter_dimension=0, tiled=True
        ).astype(jnp.float32),
    )
    placed = []
    for tensor in shards:
        rows_index = jnp.arange(2).reshape((2,) + (1,) * tensor.ndim)
        placed.append(jnp.where(rows_index == stream, tensor[None], 0.0))
    return lax.psum((placed[0], placed[1], placed[2], placed[3]), "dp")


def norm_shard(whole_rows):
    extent = whole_rows.shape[1] // lax.axis_size("blk")
    return lax.dynamic_slice_in_dim(whole_rows, lax.axis_index("blk") * extent, extent, 1)


def pool_two(values):
    clip_count, frames, height, breadth, channels = values.shape
    return values.reshape(
        clip_count, frames // 2, 2, height // 2, 2, breadth // 2, 2, channels
    ).mean(axis=(2, 4, 6))


def spread_two(upstream):
    clip_count, frames, height, breadth, channels = upstream.shape
    widened = jnp.broadcast_to(
        upstream[:, :, None, :, None, :, None, :] / 8.0,
        (clip_count, frames, 2, height, 2, breadth, 2, channels),
    )
    return widened.reshape(clip_count, frames * 2, height * 2, breadth * 2, channels)


def on_device(
    clips,
    cotangent,
    entry_4f,
    wide_4f,
    narrow_4f,
    poolproj_4f,
    gain_4f,
    shift_4f,
    entry_5b,
    wide_5b,
    narrow_5b,
    poolproj_5b,
    gain_5b,
    shift_5b,
):
    groups = lax.axis_size("dp")
    stream = lax.axis_index("dp") // (groups // 2)
    replicas = groups // 2 * lax.axis_size("blk")
    clips_here, cotangent_here = (clips, cotangent)
    params_early = (entry_4f, wide_4f, narrow_4f, poolproj_4f, gain_4f, shift_4f)
    params_late = (entry_5b, wide_5b, narrow_5b, poolproj_5b, gain_5b, shift_5b)
    weights_early = fetch_weights(params_early, stream)
    voxels_early = replicas * clips.shape[0] * clips.shape[1] * clips.shape[2] * clips.shape[3]
    out_early, kept_early = forward_layer(clips_here, weights_early, stream, voxels_early)
    middle_low = pool_two(out_early).astype(jnp.bfloat16)
    weights_late = fetch_weights(params_late, stream)
    voxels_late = voxels_early // 8
    features, kept_late = forward_layer(middle_low, weights_late, stream, voxels_late)
    back_late = refetch_weights(params_late, stream)
    grad_middle, grads_late, norms_late = backward_layer(
        cotangent_here.astype(jnp.float32), middle_low, back_late, kept_late, stream, voxels_late
    )
    back_early = refetch_weights(params_early, stream)
    grad_clips, grads_early, norms_early = backward_layer(
        spread_two(grad_middle), clips_here, back_early, kept_early, stream, voxels_early
    )
    summed_early = reduce_grads(grads_early, stream)
    summed_late = reduce_grads(grads_late, stream)
    return (
        features,
        grad_clips,
        summed_early[0],
        summed_early[1],
        summed_early[2],
        summed_early[3],
        norm_shard(norms_early[0]),
        norm_shard(norms_early[1]),
        summed_late[0],
        summed_late[1],
        summed_late[2],
        summed_late[3],
        norm_shard(norms_late[0]),
        norm_shard(norms_late[1]),
    )


def solution(mesh):
    placed = (
        P("dp", "blk", None, None, None),
        P("dp", "blk", None, None, None),
        P(None, "blk"),
        P(None, "blk"),
        P(None, "blk"),
        P(None, "blk"),
        P(None, "blk"),
        P(None, "blk"),
        P(None, "blk"),
        P(None, "blk"),
        P(None, "blk"),
        P(None, "blk"),
        P(None, "blk"),
        P(None, "blk"),
    )
    return jax.shard_map(
        on_device,
        mesh=mesh,
        in_specs=placed,
        out_specs=(
            P("dp", "blk", None, None, None),
            P("dp", "blk", None, None, None),
            P(None, "blk"),
            P(None, "blk"),
            P(None, "blk"),
            P(None, "blk"),
            P(None, "blk"),
            P(None, "blk"),
            P(None, "blk"),
            P(None, "blk"),
            P(None, "blk"),
            P(None, "blk"),
            P(None, "blk"),
            P(None, "blk"),
        ),
        check_vma=False,
    )
```

profile of v0, /device:TPU:0, one launch (start us, length us, event | category | flops | bytes accessed | tf_op | source)
XLA Modules:
  0.0 1643.4 jit_solution(17189353919234873196)
XLA Ops:
  8.2 12.6 all-gather.2
  21.4 7.6 all-gather.1
  30.2 19.3 %all-gather = bf16[1,236544]{1,0:T(2,128)(2,1)} all-gather(bf16[1,59136]{1,0:T(2,128)(2,1)S(1)} %constant_dynamic-slice_fusion.59), channel_id=2, replica_groups=mesh['dp'=8,'blk'=4] {'blk'}, dimensions={1}, use_global_device_ids=true | all-gather | bytes 591360 | tf_op jit(solution)/shard_map/all_gather | solution.py:318
  49.5 11.6 reduce.33
  65.3 38.9 %all-reduce.27 = (f32[2,448]{1,0:T(2,128)S(1)}, f32[2,448]{1,0:T(2,128)S(1)}) all-reduce(f32[2,448]{1,0:T(2,128)S(1)} %get-tuple-element.350, f32[2,448]{1,0:T(2,128)S(1)} %get-tuple-element.349), channel_id=1, replica_groups=mesh['dp'=8,'blk'=4] {'dp','blk'}, use_global_device_ids=true, to_apply=%region_3.4 | all-reduce | flops 1792 | bytes 14336 | tf_op jit(solution)/shard_map/psum | solution.py:113
  111.3 5.5 collective-permute-start
  119.4 4.0 constant_dynamic-slice_fusion.40
  124.8 24.3 %all-gather.8 = bf16[1,1024]{1,0:T(2,128)(2,1)S(1)} all-gather(bf16[1,256]{1,0:T(2,128)(2,1)S(1)} %constant_dynamic-slice_fusion.41), channel_id=10, replica_groups=mesh['dp'=8,'blk'=4] {'blk'}, dimensions={1}, use_global_device_ids=true | all-gather | bytes 2560 | tf_op jit(solution)/shard_map/all_gather | solution.py:323
  150.4 9.9 all-gather.7
  161.9 50.0 %all-gather.6 = bf16[1,372736]{1,0:T(2,128)(2,1)} all-gather(bf16[1,93184]{1,0:T(2,128)(2,1)S(1)} %constant_dynamic-slice_fusion.45), channel_id=8, replica_groups=mesh['dp'=8,'blk'=4] {'blk'}, dimensions={1}, use_global_device_ids=true | all-gather | bytes 931840 | tf_op jit(solution)/shard_map/all_gather | solution.py:318
  212.2 22.3 %all-gather.4 = bf16[1,110592]{1,0:T(2,128)(2,1)S(1)} all-gather(bf16[1,27648]{1,0:T(2,128)(2,1)S(1)} %constant_dynamic-slice_fusion.51), channel_id=6, replica_groups=mesh['dp'=8,'blk'=4] {'blk'}, dimensions={1}, use_global_device_ids=true | all-gather | bytes 276480 | tf_op jit(solution)/shard_map/all_gather | solution.py:320
  234.6 22.0 %all-gather.11 = bf16[1,106496]{1,0:T(2,128)(2,1)} all-gather(bf16[1,26624]{1,0:T(2,128)(2,1)S(1)} %constant_dynamic-slice_fusion.34), channel_id=13, replica_groups=mesh['dp'=8,'blk'=4] {'blk'}, dimensions={1}, use_global_device_ids=true | all-gather | bytes 266240 | tf_op jit(solution)/shard_map/all_gather | solution.py:321
  256.7 17.2 %all-gather.10 = bf16[1,110592]{1,0:T(2,128)(2,1)} all-gather(bf16[1,27648]{1,0:T(2,128)(2,1)S(1)} %constant_dynamic-slice_fusion.37), channel_id=12, replica_groups=mesh['dp'=8,'blk'=4] {'blk'}, dimensions={1}, use_global_device_ids=true | all-gather | bytes 276480 | tf_op jit(solution)/shard_map/all_gather | solution.py:320
  274.0 15.8 all-gather.5
  289.8 16.5 %reduce.41 = bf16[372736]{0:T(1024)(128)(2,1)S(1)} reduce(bf16[1,372736]{1,0:T(2,128)(2,1)} %all-gather.6, bf16[]{:T(256)} %constant.426), dimensions={0}, to_apply=%all-gather.6.reduce_sub_computation | reduce | bytes 1490946 | tf_op jit(solution)/shard_map/all_gather | solution.py:318
  325.7 6.6 select_maximum_fusion
  332.3 6.7 slice_convert_fusion
  366.2 8.6 fusion.982
  376.4 4.0 fusion.980
  383.8 6.7 slice_add_fusion.2
  402.6 60.4 %reduce.34 = bf16[1382400]{0:T(1024)(128)(2,1)} reduce(bf16[1,1382400]{1,0:T(2,128)(2,1)} %all-gather.15.cloned.1.call-done, bf16[]{:T(256)} %constant.426), dimensions={0}, to_apply=%all-gather.3.reduce_sub_computation | reduce | bytes 5529602 | tf_op jit(solution)/shard_map/all_gather | solution.py:319
  463.1 8.1 reshape.1186
  471.2 8.1 copy.552
  530.8 14.2 fusion.964
  545.1 41.1 %all-reduce.26 = (f32[2,128]{1,0:T(2,128)S(1)}, f32[2,128]{1,0:T(2,128)S(1)}, f32[2,128]{1,0:T(2,128)S(1)}, f32[2,128]{1,0:T(2,128)S(1)}, f32[2,320]{1,0:T(2,128)S(1)}, /*index=5*/f32[2,320]{1,0:T(2,128)S(1)}) all-reduce(f32[2,128]{1,0:T(2,128)S(1)} %get-tuple-element.348, ...), channel_id=1, replica_groups=mesh['dp'=8,'blk'=4] {'dp','blk'}, use_global_device_ids=true, to_apply=%region_15.16 | all-reduce | flops 2304 | bytes 18432 | tf_op jit(solution)/shard_map/psum | solution.py:113
  596.5 41.8 %all-reduce.25 = (f32[2,448]{1,0:T(2,128)S(1)}, f32[2,448]{1,0:T(2,128)S(1)}) all-reduce(f32[2,448]{1,0:T(2,128)S(1)} %get-tuple-element.342, f32[2,448]{1,0:T(2,128)S(1)} %get-tuple-element.341), channel_id=1, replica_groups=mesh['dp'=8,'blk'=4] {'dp','blk'}, use_global_device_ids=true, to_apply=%region_21.22 | all-reduce | flops 1792 | bytes 14336 | tf_op jit(solution)/shard_map/psum | solution.py:113
  642.9 5.3 collective-permute-start.2
  649.0 60.4 %reduce.42 = bf16[1382400]{0:T(1024)(128)(2,1)} reduce(bf16[1,1382400]{1,0:T(2,128)(2,1)} %all-gather.17.cloned.1.call-done, bf16[]{:T(256)} %constant.426), dimensions={0}, to_apply=%all-gather.9.reduce_sub_computation | reduce | bytes 5529602 | tf_op jit(solution)/shard_map/all_gather | solution.py:319
  709.4 8.1 reshape.1191
  717.5 8.1 copy.556
  744.9 37.8 %all-reduce.24 = (f32[2,128]{1,0:T(2,128)S(1)}, f32[2,128]{1,0:T(2,128)S(1)}, f32[2,128]{1,0:T(2,128)S(1)}, f32[2,128]{1,0:T(2,128)S(1)}, f32[2,320]{1,0:T(2,128)S(1)}, /*index=5*/f32[2,320]{1,0:T(2,128)S(1)}) all-reduce(f32[2,128]{1,0:T(2,128)S(1)} %get-tuple-element.340, ...), channel_id=1, replica_groups=mesh['dp'=8,'blk'=4] {'dp','blk'}, use_global_device_ids=true, to_apply=%region_33.34 | all-reduce | flops 2304 | bytes 18432 | tf_op jit(solution)/shard_map/psum | solution.py:113
  786.4 42.6 %all-reduce.23 = (f32[2,128]{1,0:T(2,128)S(1)}, f32[2,128]{1,0:T(2,128)S(1)}, f32[2,320]{1,0:T(2,128)S(1)}, f32[2,320]{1,0:T(2,128)S(1)}, f32[2,128]{1,0:T(2,128)S(1)}, /*index=5*/f32[2,128]{1,0:T(2,128)S(1)}) all-reduce(f32[2,128]{1,0:T(2,128)S(1)} %get-tuple-element.332, ...), channel_id=1, replica_groups=mesh['dp'=8,'blk'=4] {'dp','blk'}, use_global_device_ids=true, to_apply=%region_45.46 | all-reduce | flops 2304 | bytes 18432 | tf_op jit(solution)/shard_map/psum | solution.py:113
  848.2 5.6 collective-permute-start.4
  873.0 8.4 copy.684
  881.4 9.0 convert_element_type.221
  900.3 37.7 %all-reduce.22 = (f32[2,448]{1,0:T(2,128)S(1)}, f32[2,448]{1,0:T(2,128)S(1)}) all-reduce(f32[2,448]{1,0:T(2,128)S(1)} %get-tuple-element.328, f32[2,448]{1,0:T(2,128)S(1)} %get-tuple-element.327), channel_id=1, replica_groups=mesh['dp'=8,'blk'=4] {'dp','blk'}, use_global_device_ids=true, to_apply=%region_49.50 | all-reduce | flops 1792 | bytes 14336 | tf_op jit(solution)/shard_map/psum | solution.py:113
  951.1 42.6 %all-reduce.21 = (f32[2,128]{1,0:T(2,128)S(1)}, f32[2,128]{1,0:T(2,128)S(1)}, f32[2,320]{1,0:T(2,128)S(1)}, f32[2,320]{1,0:T(2,128)S(1)}, f32[2,128]{1,0:T(2,128)S(1)}, /*index=5*/f32[2,128]{1,0:T(2,128)S(1)}) all-reduce(f32[2,128]{1,0:T(2,128)S(1)} %get-tuple-element.324, ...), channel_id=1, replica_groups=mesh['dp'=8,'blk'=4] {'dp','blk'}, use_global_device_ids=true, to_apply=%region_61.62 | all-reduce | flops 2304 | bytes 18432 | tf_op jit(solution)/shard_map/psum | solution.py:113
  1066.7 18.5 %add_add_fusion = f32[8,4,8,8,160]{4,3,2,1,0:T(8,128)S(1)} fusion(f32[8,4,8,8,160]{4,3,2,1,0:T(8,128)} %fusion.55, f32[8,4,8,8,160]{4,3,2,1,0:T(8,128)} %fusion.54, f32[8,4,8,8,160]{4,3,2,1,0:T(8,128)} %fusion.53, f32[8,4,8,8,160]{4,3,2,1,0:T(8,128)} %fusion.52, f32[8,4,8,8,160]{4,3,2,1,0:T(8,128)} %fusion.51, f32[8,4,8,8,160]{4,3,2,1,0:T(8,128)} %fusion.50, ...), kind=kOutput, calls=%fused_computation.118 | convolution fusion | flops 218234880 | bytes 56614912 | tf_op jit(solution)/shard_map/nfhwc,cd->nfhwd/dot_general | solution.py:55
  1085.2 4.2 fusion.975
  1091.0 5.6 collective-permute-start.6
  1134.1 8.4 copy.625
  1142.5 9.0 convert_element_type.209
  1171.8 37.7 %all-reduce.20 = (f32[2,448]{1,0:T(2,128)S(1)}, f32[2,448]{1,0:T(2,128)S(1)}) all-reduce(f32[2,448]{1,0:T(2,128)S(1)} %get-tuple-element.320, f32[2,448]{1,0:T(2,128)S(1)} %get-tuple-element.319), channel_id=1, replica_groups=mesh['dp'=8,'blk'=4] {'dp','blk'}, use_global_device_ids=true, to_apply=%region_65.66 | all-reduce | flops 1792 | bytes 14336 | tf_op jit(solution)/shard_map/psum | solution.py:113
  1221.3 262.5 %all-reduce.35.cloned.1.call-done = (bf16[236544]{0:T(1024)(128)(2,1)}, bf16[1382400]{0:T(1024)(128)(2,1)}, bf16[110592]{0:T(1024)(128)(2,1)}, bf16[67584]{0:T(1...) async-done(((bf16[236544]{0:T(1024)(128)(2,1)}, bf16[1382400]{0:T(1024)(128)(2,1)}, ...) | async-done | bytes 7538704
  1496.0 9.2 broadcast_select_fusion
  1510.5 4.9 slice_add_fusion.4
  1515.4 109.5 %all-reduce.33.cloned.1.call-done = (f32[2,59136]{1,0:T(2,128)}, f32[2,345600]{1,0:T(2,128)}, f32[2,27648]{1,0:T(2,128)}, f32[2,16896]{1,0:T(2,128)}, f32[2,9318...) async-done(((f32[2,59136]{1,0:T(2,128)}, f32[2,345600]{1,0:T(2,128)}, f32[2,27648]{1,0:T(2,128)}, f32[2,16896]{1,0:T(2,128)}, ...) | async-done | bytes 7538704 | tf_op jit(solution)/shard_map/psum | solution.py:360
  1626.7 4.7 copy.1384
  (1075 shorter events, 397.5 us)
Async XLA Ops:
  7.2 109.6 %copy-start = (bf16[2,345600]{1,0:T(2,128)(2,1)S(1)}, bf16[2,345600]{1,0:T(2,128)(2,1)}, u32[]{:S(2)}) copy-start(bf16[2,345600]{1,0:T(2,128)(2,1)} %param.25) | copy-start | bytes 4147204
  7.2 55.7 %copy-start.7 = (bf16[8,2,8,8,528]{4,3,2,1,0:T(8,128)(2,1)S(1)}, bf16[8,2,8,8,528]{4,3,2,1,0:T(8,128)(2,1)}, u32[]{:S(2)}) copy-start(bf16[8,2,8,8,528]{4,3,2,1,0:T(8,128)(2,1)} %param.22) | copy-start | bytes 3244036
  7.2 395.4 %all-gather.15.cloned.1.call-start = ((), (), s32[]{:S(2)}) async-start(), calls=%async_computation | async-start | bytes 6912000 | tf_op jit(solution)/shard_map/all_gather | solution.py:319
  7.3 943.7 %copy-start.156 = (pred[2]{0:T(512)(128)(4,1)}, pred[2]{0:T(512)(128)(4,1)S(1)}, u32[]{:S(2)}) copy-start(pred[2]{0:T(512)(128)(4,1)S(1)} %iota_compare_fusion.8) | copy-start | bytes 10
  20.8 84.1 %copy-start.171 = (f32[1,448]{1,0:T(1,128)}, f32[1,448]{1,0:T(1,128)S(1)}, u32[]{:S(2)}) copy-start(f32[1,448]{1,0:T(1,128)S(1)} %slice.2588) | copy-start | bytes 5380
  29.0 75.8 %copy-start.163 = (f32[1,448]{1,0:T(1,128)}, f32[1,448]{1,0:T(1,128)S(1)}, u32[]{:S(2)}) copy-start(f32[1,448]{1,0:T(1,128)S(1)} %slice.2587) | copy-start | bytes 5380
  108.5 217.2 %copy-start.14 = (bf16[8,2,8,8,192]{4,3,2,1,0:T(8,128)(2,1)}, bf16[8,2,8,8,192]{4,3,2,1,0:T(8,128)(2,1)S(1)}, u32[]{:S(2)}) copy-start(bf16[8,2,8,8,192]{4,3,2,1,0:T(8,128)(2,1)S(1)} %slice.2590) | copy-start | bytes 1179652
  110.1 215.6 %collective-permute-start.1 = (bf16[8,1,8,8,720]{4,3,2,1,0:T(8,128)(2,1)}, bf16[8,1,8,8,720]{4,3,2,1,0:T(8,128)(2,1)}, u32[]{:S(2)}, u32[]{:S(2)}) collective-permute-start(bf16[8,1,8,8,720]{4,3,2,1,0:T(8,128)(2,1)} %get-tuple-element.289), channel_id=1, source_target_pairs={{1,0},{2,1},{3,2},{5,4},{6,5},{7,6},{9,8},{10,9},{11,10},{13,12},{... | collective-permute-start | bytes 2211848 | tf_op jit(solution)/shard_map/ppermute | solution.py:26
  111.3 214.3 %collective-permute-start = (bf16[8,1,8,8,720]{4,3,2,1,0:T(8,128)(2,1)}, bf16[8,1,8,8,720]{4,3,2,1,0:T(8,128)(2,1)}, u32[]{:S(2)}, u32[]{:S(2)}) collective-permute-start(bf16[8,1,8,8,720]{4,3,2,1,0:T(8,128)(2,1)} %get-tuple-element.288), channel_id=1, source_target_pairs={{0,1},{1,2},{2,3},{4,5},{5,6},{6,7},{8,9},{9,10},{10,11},{12,13},{... | collective-permute-start | bytes 2211848 | tf_op jit(solution)/shard_map/ppermute | solution.py:23
  119.4 529.6 %all-gather.17.cloned.1.call-start = ((), (), s32[]{:S(2)}) async-start(), calls=%async_computation.1 | async-start | bytes 6912000 | tf_op jit(solution)/shard_map/all_gather | solution.py:319
  123.4 88.5 %copy-start.162 = (bf16[2,16896]{1,0:T(2,128)(2,1)S(1)}, bf16[2,16896]{1,0:T(2,128)(2,1)}, u32[]{:S(2)}) copy-start(bf16[2,16896]{1,0:T(2,128)(2,1)} %param.27) | copy-start | bytes 202756
  123.4 88.6 %copy-start.159 = (bf16[2,27648]{1,0:T(2,128)(2,1)S(1)}, bf16[2,27648]{1,0:T(2,128)(2,1)}, u32[]{:S(2)}) copy-start(bf16[2,27648]{1,0:T(2,128)(2,1)} %param.26) | copy-start | bytes 331780
  123.4 111.1 %copy-start.161 = (bf16[2,26624]{1,0:T(2,128)(2,1)S(1)}, bf16[2,26624]{1,0:T(2,128)(2,1)}, u32[]{:S(2)}) copy-start(bf16[2,26624]{1,0:T(2,128)(2,1)} %param.33) | copy-start | bytes 319492
  123.5 1360.3 %all-reduce.35.cloned.1.call-start = ((), (), s32[]{:S(2)}) async-start(), calls=%async_computation.3 | async-start | bytes 15077376
  124.2 464.3 %copy-start.183 = (f32[320]{0:T(512)}, f32[320]{0:T(512)S(1)}, u32[]{:S(2)}) copy-start(f32[320]{0:T(512)S(1)} %slice_reduce_fusion.2) | copy-start | bytes 3844
  160.3 96.3 %copy-start.191 = (f32[1,1024]{1,0:T(1,128)}, f32[1,1024]{1,0:T(1,128)S(1)}, u32[]{:S(2)}) copy-start(f32[1,1024]{1,0:T(1,128)S(1)} %convert_element_type.231) | copy-start | bytes 12292
  161.5 95.1 %copy-start.160 = (bf16[2,27648]{1,0:T(2,128)(2,1)S(1)}, bf16[2,27648]{1,0:T(2,128)(2,1)}, u32[]{:S(2)}) copy-start(bf16[2,27648]{1,0:T(2,128)(2,1)} %param.32) | copy-start | bytes 331780
  289.7 349.2 %copy-start.189 = (f32[1,448]{1,0:T(1,128)}, f32[1,448]{1,0:T(1,128)S(1)}, u32[]{:S(2)}) copy-start(f32[1,448]{1,0:T(1,128)S(1)} %slice.2714) | copy-start | bytes 5380
  289.8 349.2 %copy-start.181 = (f32[1,448]{1,0:T(1,128)}, f32[1,448]{1,0:T(1,128)S(1)}, u32[]{:S(2)}) copy-start(f32[1,448]{1,0:T(1,128)S(1)} %slice.2713) | copy-start | bytes 5380
  332.3 65.7 %copy-start.2 = (bf16[8,4,10,10,720]{4,3,2,1,0:T(8,128)(2,1)}, bf16[8,4,10,10,720]{4,3,2,1,0:T(8,128)(2,1)S(1)}, u32[]{:S(2)}) copy-start(bf16[8,4,10,10,720]{4,3,2,1,0:T(8,128)(2,1)S(1)} %select_maximum_fusion) | copy-start | bytes 13824004
  402.6 125.0 %copy-start.68 = (bf16[8,2,8,8,160]{4,3,2,1,0:T(8,128)(2,1)}, bf16[8,2,8,8,160]{4,3,2,1,0:T(8,128)(2,1)S(1)}, u32[]{:S(2)}) copy-start(bf16[8,2,8,8,160]{4,3,2,1,0:T(8,128)(2,1)S(1)} %get-tuple-element.285) | copy-start | bytes 983044
  402.6 126.6 %copy-start.70 = (bf16[8,2,8,8,160]{4,3,2,1,0:T(8,128)(2,1)}, bf16[8,2,8,8,160]{4,3,2,1,0:T(8,128)(2,1)S(1)}, u32[]{:S(2)}) copy-start(bf16[8,2,8,8,160]{4,3,2,1,0:T(8,128)(2,1)S(1)} %get-tuple-element.284) | copy-start | bytes 983044
  530.8 57.3 %copy-start.197 = (f32[128]{0:T(128)S(1)}, f32[128]{0:T(128)}, u32[]{:S(2)}) copy-start(f32[128]{0:T(128)} %get-tuple-element.314) | copy-start | bytes 1540
  530.8 57.3 %copy-start.199 = (f32[128]{0:T(128)S(1)}, f32[128]{0:T(128)}, u32[]{:S(2)}) copy-start(f32[128]{0:T(128)} %get-tuple-element.312) | copy-start | bytes 1540
  530.8 57.5 %copy-start.18 = (f32[8,2,8,8,128]{4,3,2,1,0:T(8,128)S(1)}, f32[8,2,8,8,128]{4,3,2,1,0:T(8,128)}, u32[]{:S(2)}) copy-start(f32[8,2,8,8,128]{4,3,2,1,0:T(8,128)} %get-tuple-element.352) | copy-start | bytes 1572868
  530.8 57.5 %copy-start.201 = (f32[128]{0:T(128)S(1)}, f32[128]{0:T(128)}, u32[]{:S(2)}) copy-start(f32[128]{0:T(128)} %get-tuple-element.313) | copy-start | bytes 1540
  530.8 57.5 %copy-start.203 = (f32[128]{0:T(128)S(1)}, f32[128]{0:T(128)}, u32[]{:S(2)}) copy-start(f32[128]{0:T(128)} %get-tuple-element.311) | copy-start | bytes 1540
  595.0 53.2 %copy-start.77 = (bf16[128,27,32]{0,2,1:T(8,128)(2,1)S(1)}, bf16[128,27,32]{0,2,1:T(8,128)(2,1)}, u32[]{:S(2)}) copy-start(bf16[128,27,32]{0,2,1:T(8,128)(2,1)} %copy.557) | copy-start | bytes 663556
  638.9 70.5 %copy-start.179 = (f32[448]{0:T(512)}, f32[448]{0:T(512)S(1)}, u32[]{:S(2)}) copy-start(f32[448]{0:T(512)S(1)} %get-tuple-element.300) | copy-start | bytes 5380
  639.7 85.9 %copy-start.95 = (bf16[8,1,4,4,448]{4,0,3,2,1:T(8,128)(2,1)}, bf16[8,1,4,4,448]{4,0,3,2,1:T(8,128)(2,1)S(1)}, u32[]{:S(2)}) copy-start(bf16[8,1,4,4,448]{4,0,3,2,1:T(8,128)(2,1)S(1)} %get-tuple-element.228) | copy-start | bytes 344068
  641.6 85.0 %collective-permute-start.3 = (bf16[8,1,4,4,1024]{4,0,3,2,1:T(8,128)(2,1)}, bf16[8,1,4,4,1024]{4,0,3,2,1:T(8,128)(2,1)S(1)}, u32[]{:S(2)}, u32[]{:S(2)}) collective-permute-start(bf16[8,1,4,4,1024]{4,0,3,2,1:T(8,128)(2,1)} %pad_maximum_fusion.16), channel_id=1, source_target_pairs={{1,0},{2,1},{3,2},{5,4},{6,5},{7,6},{9,8},{10,9},{11,10},{13,12},{... | collective-permute-start | bytes 786440 | tf_op jit(solution)/shard_map/ppermute | solution.py:26
  642.9 83.8 %collective-permute-start.2 = (bf16[8,1,4,4,1024]{4,0,3,2,1:T(8,128)(2,1)}, bf16[8,1,4,4,1024]{4,0,3,2,1:T(8,128)(2,1)}, u32[]{:S(2)}, u32[]{:S(2)}) collective-permute-start(bf16[8,1,4,4,1024]{4,0,3,2,1:T(8,128)(2,1)} %pad_maximum_fusion.16), channel_id=1, source_target_pairs={{0,1},{1,2},{2,3},{4,5},{5,6},{6,7},{8,9},{9,10},{10,11},{12,13},{... | collective-permute-start | bytes 786440 | tf_op jit(solution)/shard_map/ppermute | solution.py:23
  739.3 104.5 %copy-start.87 = (f32[8,4,4,128]{3,0,2,1:T(8,128)}, f32[8,4,4,128]{3,0,2,1:T(8,128)S(1)}, u32[]{:S(2)}) copy-start(f32[8,4,4,128]{3,0,2,1:T(8,128)S(1)} %get-tuple-element.357) | copy-start | bytes 196612
  742.3 92.4 %copy-start.35 = (f32[8,4,4,320]{3,0,2,1:T(8,128)}, f32[8,4,4,320]{3,0,2,1:T(8,128)S(1)}, u32[]{:S(2)}) copy-start(f32[8,4,4,320]{3,0,2,1:T(8,128)S(1)} %get-tuple-element.358) | copy-start | bytes 491524
  744.8 86.5 %copy-start.85 = (f32[8,4,4,128]{3,0,2,1:T(8,128)}, f32[8,4,4,128]{3,0,2,1:T(8,128)S(1)}, u32[]{:S(2)}) copy-start(f32[8,4,4,128]{3,0,2,1:T(8,128)S(1)} %get-tuple-element.356) | copy-start | bytes 196612
  782.7 61.1 %copy-start.224 = (f32[128]{0:T(128)}, f32[128]{0:T(128)S(1)}, u32[]{:S(2)}) copy-start(f32[128]{0:T(128)S(1)} %fusion.776) | copy-start | bytes 1540
  782.8 51.9 %copy-start.167 = (f32[320]{0:T(512)}, f32[320]{0:T(512)S(1)}, u32[]{:S(2)}) copy-start(f32[320]{0:T(512)S(1)} %fusion.749) | copy-start | bytes 3844
  784.0 59.8 %copy-start.207 = (f32[128]{0:T(128)}, f32[128]{0:T(128)S(1)}, u32[]{:S(2)}) copy-start(f32[128]{0:T(128)S(1)} %get-tuple-element.304) | copy-start | bytes 1540
  784.0 50.7 %copy-start.175 = (f32[320]{0:T(512)}, f32[320]{0:T(512)S(1)}, u32[]{:S(2)}) copy-start(f32[320]{0:T(512)S(1)} %get-tuple-element.302) | copy-start | bytes 3844
  846.9 49.4 %collective-permute-start.5 = (bf16[8,1,4,4,1024]{4,0,3,2,1:T(8,128)(2,1)}, bf16[8,1,4,4,1024]{4,0,3,2,1:T(8,128)(2,1)}, u32[]{:S(2)}, u32[]{:S(2)}) collective-permute-start(bf16[8,1,4,4,1024]{4,0,3,2,1:T(8,128)(2,1)} %get-tuple-element.291), channel_id=1, source_target_pairs={{1,0},{2,1},{3,2},{5,4},{6,5},{7,6},{9,8},{10,9},{11,10},{13,12},{... | collective-permute-start | bytes 786440 | tf_op jit(solution)/shard_map/ppermute | solution.py:26
  848.2 48.1 %collective-permute-start.4 = (bf16[8,1,4,4,1024]{4,0,3,2,1:T(8,128)(2,1)}, bf16[8,1,4,4,1024]{4,0,3,2,1:T(8,128)(2,1)}, u32[]{:S(2)}, u32[]{:S(2)}) collective-permute-start(bf16[8,1,4,4,1024]{4,0,3,2,1:T(8,128)(2,1)} %get-tuple-element.290), channel_id=1, source_target_pairs={{0,1},{1,2},{2,3},{4,5},{5,6},{6,7},{8,9},{9,10},{10,11},{12,13},{... | collective-permute-start | bytes 786440 | tf_op jit(solution)/shard_map/ppermute | solution.py:23
  993.7 57.2 %copy-start.251 = (f32[2,128]{1,0:T(2,128)}, f32[2,128]{1,0:T(2,128)S(1)}, u32[]{:S(2)}) copy-start(f32[2,128]{1,0:T(2,128)S(1)} %get-tuple-element.166) | copy-start | bytes 3076
  993.7 57.2 %copy-start.247 = (f32[2,128]{1,0:T(2,128)}, f32[2,128]{1,0:T(2,128)S(1)}, u32[]{:S(2)}) copy-start(f32[2,128]{1,0:T(2,128)S(1)} %get-tuple-element.167) | copy-start | bytes 3076
  993.7 66.7 %copy-start.253 = (f32[2,128]{1,0:T(2,128)}, f32[2,128]{1,0:T(2,128)S(1)}, u32[]{:S(2)}) copy-start(f32[2,128]{1,0:T(2,128)S(1)} %get-tuple-element.170) | copy-start | bytes 3076
  993.8 66.7 %copy-start.249 = (f32[2,128]{1,0:T(2,128)}, f32[2,128]{1,0:T(2,128)S(1)}, u32[]{:S(2)}) copy-start(f32[2,128]{1,0:T(2,128)S(1)} %get-tuple-element.171) | copy-start | bytes 3076
  1089.5 73.1 %collective-permute-start.7 = (bf16[8,1,8,8,720]{4,3,2,1,0:T(8,128)(2,1)S(1)}, bf16[8,1,8,8,720]{4,3,2,1,0:T(8,128)(2,1)}, u32[]{:S(2)}, u32[]{:S(2)}) collective-permute-start(bf16[8,1,8,8,720]{4,3,2,1,0:T(8,128)(2,1)S(1)} %get-tuple-element.281), channel_id=1, source_target_pairs={{1,0},{2,1},{3,2},{5,4},{6,5},{7,6},{9,8},{10,9},{11,10},{13,12},{... | collective-permute-start | bytes 2211848 | tf_op jit(solution)/shard_map/ppermute | solution.py:26
  1091.0 71.7 %collective-permute-start.6 = (bf16[8,1,8,8,720]{4,3,2,1,0:T(8,128)(2,1)S(1)}, bf16[8,1,8,8,720]{4,3,2,1,0:T(8,128)(2,1)}, u32[]{:S(2)}, u32[]{:S(2)}) collective-permute-start(bf16[8,1,8,8,720]{4,3,2,1,0:T(8,128)(2,1)S(1)} %get-tuple-element.280), channel_id=1, source_target_pairs={{0,1},{1,2},{2,3},{4,5},{5,6},{6,7},{8,9},{9,10},{10,11},{12,13},{... | collective-permute-start | bytes 2211848 | tf_op jit(solution)/shard_map/ppermute | solution.py:23
  1216.2 408.7 %all-reduce.33.cloned.1.call-start = ((), (), s32[]{:S(2)}) async-start(), calls=%async_computation.2 | async-start | bytes 15077376 | tf_op jit(solution)/shard_map/psum | solution.py:360
  (229 other events, 1240.6 us)
Sparse Core Ops, SparseCore 0:
  119.5 146.1 all-gather.14
  267.2 106.5 all-gather.16
  1216.3 267.4 all-reduce.34
  1506.4 118.3 all-reduce.32
where the time goes:
time: 1660 us; the launch traced here: 1640 us
  blocking collectives  521 us (31%)
  waiting for transfers between devices  372 us (22%)
  matrix products  260 us (16%)
  other arithmetic  258 us (16%)
  local copies, waits for them, and re-layouts  181 us (11%)
  starting transfers between devices  27.7 us (2%)
  between operations  22.7 us (1%)
    psum x8, blocking collectives, share_sums(): lax.psum((place_row(couple[0], stream), place_row(couple[1], stream)), ('...  320 us
    unnamed x5, waiting for transfers between devices  263 us
    dot_general x208, matrix products, conv_taps(): jnp.einsum('nfhwc,cd->nfhwd', window(padded, tap_index, frames, height, b...  201 us
    all_gather x2, other arithmetic, fetch_weights(): lax.all_gather(own_shards[1], 'blk', axis=0, tiled=True)  121 us
    psum x1, waiting for transfers between devices, reduce_grads(): return lax.psum((placed[0], placed[1], placed[2], placed[3]), 'dp')  109 us
    all_gather x2, blocking collectives, fetch_weights(): lax.all_gather(own_shards[0], 'blk', axis=0, tiled=True)  69.3 us
    unnamed x538, local copies, waits for them, and re-layouts  40.3 us
    all_gather x2, blocking collectives, fetch_weights(): lax.all_gather(own_shards[2], 'blk', axis=0, tiled=True)  39.5 us
  transfers between devices with their start and end apart: 12, of which 2 were waited for; matrix products, arithmetic and copies ran while one was open for 28% of the time, Pallas kernels for 0%

commit v1 on v0

v1 whole, which is shorter than its diff:
```python
import jax
import jax.numpy as jnp
from jax import lax
from jax.sharding import PartitionSpec as P

B0 = 256
B1R = 160
B1 = 320
B2R = 32
B2 = 128
BP = 128
INNER = B1R + B2R
REDUCED = B0 + INNER
OUTER = B1 + B2
EPS = 1e-05
BF = jnp.bfloat16
F32 = jnp.float32
DIMS = ("NDHWC", "DHWIO", "NDHWC")
SAME = ((1, 1), (1, 1), (1, 1))


def xor_pairs(axis, step):
    return [(i, i ^ step) for i in range(lax.axis_size(axis))]


def tower_steps():
    steps, step = [], 1
    while step < lax.axis_size("dp") // 2:
        steps.append(step)
        step *= 2
    return steps


def other_tower(value):
    return lax.ppermute(value, "dp", xor_pairs("dp", lax.axis_size("dp") // 2))


def blk_peers(value):
    count = lax.axis_size("blk")
    return [value] + [lax.ppermute(value, "blk", xor_pairs("blk", k)) for k in range(1, count)]


def by_place(parts):
    me, step = lax.axis_index("blk"), 1
    while step < len(parts):
        hit = (me & step) != 0
        parts = [jnp.where(hit, parts[k ^ step], parts[k]) for k in range(len(parts))]
        step *= 2
    return parts


def gather_blk(value):
    return by_place(blk_peers(value))


def exchange_blk(chunks):
    mine = by_place(chunks)
    return [mine[0]] + [
        lax.ppermute(mine[k], "blk", xor_pairs("blk", k)) for k in range(1, len(mine))
    ]


def dp_sum(value):
    for step in tower_steps():
        value = value + lax.ppermute(value, "dp", xor_pairs("dp", step))
    return value


def blk_sum(value):
    parts = blk_peers(value)
    while len(parts) > 1:
        parts = [parts[i] + parts[i + 1] for i in range(0, len(parts), 2)]
    return parts[0]


def tower_sum(value):
    return blk_sum(dp_sum(value))


def gather_shared(shard):
    rows = shard.shape[0] // 2
    odd = lax.axis_index("dp") % 2
    half = lax.dynamic_slice_in_dim(shard, odd * rows, rows, 0)
    whole = jnp.stack(gather_blk(half))
    twin = lax.ppermute(whole, "dp", xor_pairs("dp", 1))
    low = jnp.where(odd == 0, whole, twin)
    high = jnp.where(odd == 0, twin, whole)
    return jnp.concatenate([low, high], axis=1)


def frame_halo(value):
    count = lax.axis_size("blk")
    ahead = [(i, i + 1) for i in range(count - 1)]
    back = [(i + 1, i) for i in range(count - 1)]
    before = lax.ppermute(value[:, -1:], "blk", ahead)
    after = lax.ppermute(value[:, :1], "blk", back)
    return before, after


def conv(values, kernel, pads):
    return lax.conv_general_dilated(
        values, kernel, (1, 1, 1), pads, dimension_numbers=DIMS, preferred_element_type=F32
    )


def weight_grad(values, grad, pads):
    return lax.conv_general_dilated(
        values,
        grad,
        (1, 1, 1),
        pads,
        dimension_numbers=("CDHWN", "IDHWO", "DHWNC"),
        preferred_element_type=F32,
    )


def pool_rows(padded):
    v = padded.astype(F32)
    v = v[:, :-2] + v[:, 1:-1] + v[:, 2:]
    for axis in (2, 3):
        pads = [(0, 0)] * 5
        pads[axis] = (1, 1)
        v = jnp.pad(v, pads)
        size = v.shape[axis]
        v = (
            lax.slice_in_dim(v, 0, size - 2, axis=axis)
            + lax.slice_in_dim(v, 1, size - 1, axis=axis)
            + lax.slice_in_dim(v, 2, size, axis=axis)
        )
    return v / 27.0


def moments(value):
    return jnp.stack([jnp.sum(value, (0, 1, 2, 3)), jnp.sum(value * value, (0, 1, 2, 3))])


def cross(grad, scaled):
    return jnp.stack([jnp.sum(grad, (0, 1, 2, 3)), jnp.sum(grad * scaled, (0, 1, 2, 3))])


def scale_of(sums, voxels):
    centre = sums[0] / voxels
    return centre, lax.rsqrt(sums[1] / voxels - centre * centre + EPS)


def silu_slope(y):
    sigmoid = jax.nn.sigmoid(y)
    return sigmoid * (1.0 + y * (1.0 - sigmoid))


def norm_back(dy, scaled, spread, gain, sums, voxels):
    return (gain * spread * (dy - sums[0] / voxels - scaled * (sums[1] / voxels))).astype(BF)


def block_kernel(wide, narrow):
    o, p = wide.shape[0], narrow.shape[0]
    wide = wide.reshape(o, 27, B1R).transpose(1, 2, 0)
    narrow = narrow.reshape(p, 27, B2R).transpose(1, 2, 0)
    wide = jnp.pad(wide, ((0, 0), (0, B2R), (0, p)))
    narrow = jnp.pad(narrow, ((0, 0), (B1R, 0), (o, 0)))
    return (wide + narrow).reshape(3, 3, 3, INNER, o + p)


def flip(kernel):
    return jnp.swapaxes(kernel, 3, 4)[::-1, ::-1, ::-1]


def kernel_rows(grad, o):
    grad = grad.reshape(27, INNER, grad.shape[-1])
    wide = grad[:, :B1R, :o].transpose(2, 0, 1)
    narrow = grad[:, B1R:, o:].transpose(2, 0, 1)
    return wide.reshape(wide.shape[0], -1), narrow.reshape(narrow.shape[0], -1)


def reduce_rows(part):
    steps = tower_steps()
    halved = []
    value = part.astype(BF)
    axis = value.ndim - 2
    for number, step in enumerate(steps):
        if number < 2:
            rows = value.shape[axis] // 2
            high = (lax.axis_index("dp") & step) != 0
            keep = lax.dynamic_slice_in_dim(value, jnp.where(high, rows, 0), rows, axis)
            give = lax.dynamic_slice_in_dim(value, jnp.where(high, 0, rows), rows, axis)
            halved.append(step)
        else:
            keep = give = value
        got = lax.ppermute(give, "dp", xor_pairs("dp", step))
        value = (keep.astype(F32) + got.astype(F32)).astype(BF)
    return value, halved


def spread_rows(value, halved):
    stream = lax.axis_index("dp") // (lax.axis_size("dp") // 2)
    other = other_tower(value)
    both = jnp.where(stream == 0, jnp.stack([value, other]), jnp.stack([other, value]))
    for step in reversed(halved):
        got = lax.ppermute(both, "dp", xor_pairs("dp", step))
        high = (lax.axis_index("dp") & step) != 0
        both = jnp.where(
            high, jnp.concatenate([got, both], 1), jnp.concatenate([both, got], 1)
        )
    return both.astype(F32)


def reduce_own(part):
    value, halved = reduce_rows(part)
    return spread_rows(value, halved)


def reduce_blk(part):
    value, halved = reduce_rows(part)
    got = exchange_blk([value[j] for j in range(value.shape[0])])
    total = got[0].astype(F32)
    for piece in got[1:]:
        total = total + piece.astype(F32)
    return spread_rows(total.astype(BF), halved)


def on_device(clips, cotangent, *params):
    groups = lax.axis_size("dp")
    count = lax.axis_size("blk")
    stream = lax.axis_index("dp") // (groups // 2)
    place = lax.axis_index("blk")
    own = [lax.dynamic_index_in_dim(p, stream, 0, keepdims=False) for p in params]
    early, late = own[:6], own[6:]
    n, frames, height, breadth, c_first = clips.shape
    voxels = groups // 2 * count * n * frames * height * breadth
    voxels_late = voxels // 8
    c_in = cotangent.shape[4]

    def pack_front(layer, c):
        norms = jnp.concatenate([layer[4], layer[5]])
        row = jnp.pad(norms, (0, c - norms.shape[0])).reshape(1, c)
        rows = jnp.concatenate([layer[0].reshape(-1, c), layer[3].reshape(-1, c), row])
        return jnp.pad(rows, ((0, -rows.shape[0] % 32), (0, 0)))

    def unpack_front(whole):
        e, p = REDUCED // count, BP // count
        entry = whole[:, :e].reshape(REDUCED, -1)
        pool = whole[:, e : e + p].reshape(BP, -1)
        g = (REDUCED + OUTER + BP) // count
        gain = whole[:, e + p, :g].reshape(-1).astype(F32)
        shift = whole[:, e + p, g : 2 * g].reshape(-1).astype(F32)
        return jnp.concatenate([entry, pool]), gain, shift

    own_wide = B1 // count
    own_narrow = B2 // count
    own_cols = own_wide + own_narrow

    front_4, gain_4, shift_4 = unpack_front(gather_shared(pack_front(early, c_first)))
    wide_4 = gather_shared(early[1].reshape(own_wide, -1)).reshape(B1, -1)
    narrow_4 = gather_shared(early[2].reshape(own_narrow, -1)).reshape(B2, -1)
    kernel_4 = block_kernel(wide_4, narrow_4)
    front_5, gain_5, shift_5 = unpack_front(gather_shared(pack_front(late, c_in)))
    kernel_5 = block_kernel(late[1].reshape(own_wide, -1), late[2].reshape(own_narrow, -1))

    def cols_of(value, j):
        return jnp.concatenate(
            [
                value[..., B0 + j * own_wide : B0 + (j + 1) * own_wide],
                value[..., B0 + B1 + j * own_narrow : B0 + B1 + (j + 1) * own_narrow],
            ],
            axis=-1,
        )

    cot_own = by_place(exchange_blk([cols_of(cotangent, j) for j in range(count)]))
    cot_own = jnp.concatenate(cot_own, axis=1)

    def own_norms(vector):
        wide = lax.dynamic_slice_in_dim(vector, REDUCED + place * own_wide, own_wide, 0)
        narrow = lax.dynamic_slice_in_dim(vector, REDUCED + B1 + place * own_narrow, own_narrow, 0)
        return jnp.concatenate([wide, narrow])

    product = jnp.einsum("nfhwc,oc->nfhwo", clips, front_4, preferred_element_type=F32)
    front, pre_pool = product[..., :REDUCED], product[..., REDUCED:]
    centre_f4, spread_f4 = scale_of(tower_sum(moments(front)), voxels)
    before, after = frame_halo(pre_pool.astype(BF))
    pool_out = pool_rows(jnp.concatenate([before.astype(F32), pre_pool, after.astype(F32)], 1))
    scaled_f4 = (front - centre_f4) * spread_f4
    act = jax.nn.silu(scaled_f4 * gain_4[:REDUCED] + shift_4[:REDUCED])
    inner = act[..., B0:].astype(BF)
    before, after = frame_halo(inner)
    inner_pad = jnp.concatenate([before, inner, after], 1)
    branch = jnp.concatenate([conv(inner_pad, kernel_4, ((0, 0), (1, 1), (1, 1))), pool_out], 4)
    centre_b4, spread_b4 = scale_of(tower_sum(moments(branch)), voxels)
    scaled_b4 = (branch - centre_b4) * spread_b4
    y_b4 = scaled_b4 * gain_4[REDUCED:] + shift_4[REDUCED:]
    layer = jnp.concatenate([act[..., :B0], jax.nn.silu(y_b4)], 4)
    middle = layer.reshape(n, frames // 2, 2, height // 2, 2, breadth // 2, 2, c_in)
    middle = middle.mean(axis=(2, 4, 6)).astype(BF)

    product5 = jnp.einsum("nfhwc,oc->nfhwo", middle, front_5, preferred_element_type=F32)
    front5, pre_pool5 = product5[..., :REDUCED], product5[..., REDUCED:]
    before, after = frame_halo(pre_pool5.astype(BF))
    pool_out5 = pool_rows(jnp.concatenate([before.astype(F32), pre_pool5, after.astype(F32)], 1))
    centre_f5, spread_f5 = scale_of(tower_sum(moments(front5)), voxels_late)
    scaled_f5 = (front5 - centre_f5) * spread_f5
    y_f5 = scaled_f5 * gain_5[:REDUCED] + shift_5[:REDUCED]
    act5 = jax.nn.silu(y_f5)
    inner5 = jnp.concatenate(gather_blk(act5[..., B0:].astype(BF)), axis=1)
    pool_sums5 = blk_sum(moments(pool_out5))
    conv5 = conv(inner5, kernel_5, SAME)
    sums5 = dp_sum(jnp.concatenate([moments(conv5), pool_sums5], axis=1))
    gain_c5, shift_c5 = own_norms(gain_5), own_norms(shift_5)
    centre_c5, spread_c5 = scale_of(sums5[:, :own_cols], voxels_late)
    scaled_c5 = (conv5 - centre_c5) * spread_c5
    y_c5 = scaled_c5 * gain_c5 + shift_c5
    centre_p5, spread_p5 = scale_of(sums5[:, own_cols:], voxels_late)
    gain_p5, shift_p5 = gain_5[REDUCED + OUTER :], shift_5[REDUCED + OUTER :]
    scaled_p5 = (pool_out5 - centre_p5) * spread_p5
    y_p5 = scaled_p5 * gain_p5 + shift_p5

    dy_c5 = cot_own.astype(F32) * silu_slope(y_c5)
    dy_p5 = cotangent[..., B0 + OUTER :].astype(F32) * silu_slope(y_p5)
    back5 = dp_sum(jnp.concatenate([cross(dy_c5, scaled_c5), cross(dy_p5, scaled_p5)], axis=1))
    back_c5 = back5[:, :own_cols]
    back_p5 = blk_sum(back5[:, own_cols:])
    grad_c5 = norm_back(dy_c5, scaled_c5, spread_c5, gain_c5, back_c5, voxels_late)
    part5 = conv(grad_c5, flip(kernel_5), SAME)
    got = exchange_blk([part5[:, j : j + 1].astype(BF) for j in range(count)])
    inner_grad5 = got[0].astype(F32)
    for piece in got[1:]:
        inner_grad5 = inner_grad5 + piece.astype(F32)
    grad_p5 = norm_back(dy_p5, scaled_p5, spread_p5, gain_p5, back_p5, voxels_late)
    before, after = frame_halo(grad_p5)
    pool_back5 = pool_rows(jnp.concatenate([before, grad_p5, after], 1)).astype(BF)
    dy_f5 = jnp.concatenate(
        [cotangent[..., :B0].astype(F32), inner_grad5], 4
    ) * silu_slope(y_f5)
    placed = jnp.where(jnp.arange(count)[:, None, None] == place, back_c5[None], 0.0)
    placed = jnp.where(lax.axis_index("dp") % (groups // 2) == 0, placed, 0.0)
    placed = placed.transpose(1, 0, 2).reshape(2, -1)
    front_back5 = tower_sum(jnp.concatenate([cross(dy_f5, scaled_f5), placed], axis=1))
    back_all5 = front_back5[:, REDUCED:].reshape(2, count, own_cols)
    norms_5 = jnp.concatenate(
        [
            front_back5[:, :REDUCED],
            back_all5[:, :, :own_wide].reshape(2, -1),
            back_all5[:, :, own_wide:].reshape(2, -1),
            back_p5,
        ],
        axis=1,
    )
    grad_f5 = norm_back(
        dy_f5, scaled_f5, spread_f5, gain_5[:REDUCED], front_back5[:, :REDUCED], voxels_late
    )
    grad_front5 = jnp.concatenate([grad_f5, pool_back5], 4)
    grad_middle = jnp.einsum("nfhwo,oc->nfhwc", grad_front5, front_5, preferred_element_type=F32)
    front_grad_5 = jnp.einsum("nfhwo,nfhwc->oc", grad_front5, middle, preferred_element_type=F32)
    wide_grad_5, narrow_grad_5 = kernel_rows(weight_grad(inner5, grad_c5, SAME), own_wide)

    up = jnp.broadcast_to(
        grad_middle[:, :, None, :, None, :, None, :] * 0.125,
        (n, frames // 2, 2, height // 2, 2, breadth // 2, 2, c_in),
    ).reshape(n, frames, height, breadth, c_in)
    dy_b4 = up[..., B0:] * silu_slope(y_b4)
    back_b4 = tower_sum(cross(dy_b4, scaled_b4))
    grad_b4 = norm_back(dy_b4, scaled_b4, spread_b4, gain_4[REDUCED:], back_b4, voxels)
    grad_c4, grad_p4 = grad_b4[..., :OUTER], grad_b4[..., OUTER:]
    turned = flip(kernel_4)
    flat_pads = ((0, 0), (1, 1), (1, 1))
    to_before = conv(grad_c4[:, :1], turned[2:], flat_pads).astype(BF)
    to_after = conv(grad_c4[:, -1:], turned[:1], flat_pads).astype(BF)
    ahead = [(i, i + 1) for i in range(count - 1)]
    back = [(i + 1, i) for i in range(count - 1)]
    from_after = lax.ppermute(to_before, "blk", back)
    from_before = lax.ppermute(to_after, "blk", ahead)
    before, after = frame_halo(grad_p4)
    pool_back4 = pool_rows(jnp.concatenate([before, grad_p4, after], 1)).astype(BF)
    inner_grad = conv(grad_c4, turned, SAME)
    inner_grad = inner_grad.at[:, :1].add(from_before.astype(F32))
    inner_grad = inner_grad.at[:, -1:].add(from_after.astype(F32))
    wide_grad_4, narrow_grad_4 = kernel_rows(weight_grad(inner_pad, grad_c4, flat_pads), B1)
    dy_f4 = jnp.concatenate([up[..., :B0], inner_grad], 4) * silu_slope(
        scaled_f4 * gain_4[:REDUCED] + shift_4[:REDUCED]
    )
    back_f4 = tower_sum(cross(dy_f4, scaled_f4))
    norms_4 = jnp.concatenate([back_f4, back_b4], axis=1)
    grad_f4 = norm_back(dy_f4, scaled_f4, spread_f4, gain_4[:REDUCED], back_f4, voxels)
    grad_front4 = jnp.concatenate([grad_f4, pool_back4], 4)
    clips_grad = jnp.einsum("nfhwo,oc->nfhwc", grad_front4, front_4, preferred_element_type=F32)
    front_grad_4 = jnp.einsum("nfhwo,nfhwc->oc", grad_front4, clips, preferred_element_type=F32)

    feat_c = jax.nn.silu(y_c5).astype(BF)
    got = by_place(exchange_blk([feat_c[:, j : j + 1] for j in range(count)]))
    features = jnp.concatenate(
        [act5[..., :B0]]
        + [g[..., :own_wide].astype(F32) for g in got]
        + [g[..., own_wide:].astype(F32) for g in got]
        + [jax.nn.silu(y_p5)],
        axis=4,
    )

    def split_front(grad, c):
        entry = grad[:REDUCED].reshape(count, -1, c)
        pool = grad[REDUCED:].reshape(count, -1, c)
        return jnp.concatenate([entry, pool], axis=1)

    def flat(value):
        return value.reshape(2, -1)

    e = REDUCED // count
    sum_wide_5 = reduce_own(wide_grad_5)
    sum_narrow_5 = reduce_own(narrow_grad_5)
    sum_front_5 = reduce_blk(split_front(front_grad_5, c_in))
    sum_wide_4 = reduce_blk(wide_grad_4.reshape(count, own_wide, -1))
    sum_narrow_4 = reduce_blk(narrow_grad_4.reshape(count, own_narrow, -1))
    sum_front_4 = reduce_blk(split_front(front_grad_4, c_first))

    norms = jnp.stack([norms_4, norms_5])
    theirs = other_tower(norms)
    norms = jnp.where(stream == 0, jnp.stack([norms, theirs]), jnp.stack([theirs, norms]))
    extent = norms.shape[-1] // count
    norms = lax.dynamic_slice_in_dim(norms, place * extent, extent, 3)
    return (
        features,
        clips_grad,
        flat(sum_front_4[:, :e]),
        flat(sum_wide_4),
        flat(sum_narrow_4),
        flat(sum_front_4[:, e:]),
        norms[:, 0, 1],
        norms[:, 0, 0],
        flat(sum_front_5[:, :e]),
        flat(sum_wide_5),
        flat(sum_narrow_5),
        flat(sum_front_5[:, e:]),
        norms[:, 1, 1],
        norms[:, 1, 0],
    )


def solution(mesh):
    spec = P("dp", "blk", None, None, None)
    flat = P(None, "blk")
    return jax.shard_map(
        on_device,
        mesh=mesh,
        in_specs=(spec, spec) + (flat,) * 12,
        out_specs=(spec, spec) + (flat,) * 12,
        check_vma=False,
    )
```

time: 1660 us -> 601 us (0.36)
  blocking collectives: 521 us -> 0 us
  waiting for transfers between devices: 372 us -> 96.3 us
  matrix products: 260 us -> 47 us
  other arithmetic: 258 us -> 95 us
  starting transfers between devices: 27.7 us -> 159 us
  between operations: 22.7 us -> 3.79 us
    psum x8 -> x0, blocking collectives: 320 us -> none  [share_sums(): lax.psum((place_row(couple[0], stream), place_row(couple[1], stream)), ('...]
    unnamed x5 -> x0, waiting for transfers between devices: 263 us -> none
    dot_general x336 -> x6, matrix products: 260 us -> 9.38 us  [the longest x1 2.91 us: on_device(): jnp.einsum('nfhwo,oc->nfhwc', grad_front4, front_4, preferred_element_typ...]
    all_gather x10 -> x0, blocking collectives: 201 us -> none  [the longest x2 69.3 us: fetch_weights(): lax.all_gather(own_shards[0], 'blk', axis=0, tiled=True)]
    all_gather x8 -> x0, other arithmetic: 155 us -> none  [the longest x2 121 us: fetch_weights(): lax.all_gather(own_shards[1], 'blk', axis=0, tiled=True)]
    ppermute x8 -> x123, starting transfers between devices: 27.2 us -> 159 us  [the longest x39 61.5 us: blk_peers(): lax.ppermute(value, 'blk', xor_pairs('blk', k))]
    psum x1 -> x0, waiting for transfers between devices: 109 us -> none  [reduce_grads(): return lax.psum((placed[0], placed[1], placed[2], placed[3]), 'dp')]
    ppermute x8 -> x123, waiting for transfers between devices: 0.02 us -> 96.3 us  [the longest x39 31.8 us: blk_peers(): lax.ppermute(value, 'blk', xor_pairs('blk', k))]
  transfers between devices with their start and end apart: 12 -> 123, of which waited for: 2 -> 43; matrix products, arithmetic and copies ran while one was open for 28% -> 52% of each run, Pallas kernels for 0% -> 0%
where the time goes in v1:
time: 601 us; the launch traced here: 591 us
  local copies, waits for them, and re-layouts  190 us (32%)
  starting transfers between devices  159 us (26%)
  waiting for transfers between devices  96.3 us (16%)
  other arithmetic  95 us (16%)
  matrix products  47 us (8%)
    ppermute x39, starting transfers between devices, blk_peers(): lax.ppermute(value, 'blk', xor_pairs('blk', k))  61.5 us
    ppermute x39, waiting for transfers between devices, blk_peers(): lax.ppermute(value, 'blk', xor_pairs('blk', k))  31.8 us
    ppermute x21, starting transfers between devices, exchange_blk(): lax.ppermute(mine[k], 'blk', xor_pairs('blk', k))  31.7 us
    unnamed x281, local copies, waits for them, and re-layouts  25.1 us
    dynamic_slice x8, local copies, waits for them, and re-layouts, on_device(): lax.dynamic_index_in_dim(p, stream, 0, keepdims=False)  24.8 us
    conv_general_dilated x6, matrix products, conv(): lax.conv_general_dilated(values, kernel, (1, 1, 1), pads, dimension_numbe...  24.6 us
    ppermute x5, starting transfers between devices, frame_halo(): before = lax.ppermute(value[:, -1:], 'blk', ahead)  21.8 us
    another operation x3, local copies, waits for them, and re-layouts, block_kernel(): wide = wide.reshape(o, 27, B1R).transpose(1, 2, 0)  21.3 us
  transfers between devices with their start and end apart: 123, of which 43 were waited for; matrix products, arithmetic and copies ran while one was open for 52% of the time, Pallas kernels for 0%

profile of v1, /device:TPU:0, one launch (start us, length us, event | category | flops | bytes accessed | tf_op | source)
XLA Modules:
  0.0 591.0 jit_solution(8628600736742374770)
XLA Ops:
  3.9 3.0 collective-permute-start.17
  14.5 3.5 collective-permute-start.1
  30.5 16.6 %dynamic-slice_reduce_fusion = (bf16[345600]{0:T(1024)(128)(2,1)}, bf16[345600]{0:T(1024)(128)(2,1)S(1)}) fusion(bf16[2,345600]{1,0:T(2,128)(2,1)S(1)} %copy-done.20, s32[]{:T(128)S(6)} %select_n.991, bf16[2,345600]{1,0:T(2,128)(2,1)} %param.21), kind=kLoop, calls=%fused_computation.41 | loop fusion | bytes 2764804 | tf_op jit(solution)/shard_map/jit(dynamic_index_in_dim)/dynamic_slice | solution.py:226
  51.9 3.8 collective-permute-start.27
  69.5 3.5 collective-permute-start.50
  76.0 18.0 %collective-permute-done.12 = bf16[40,4320]{1,0:T(8,128)(2,1)} collective-permute-done((bf16[40,4320]{1,0:T(8,128)(2,1)}, bf16[40,4320]{1,0:T(8,128)(2,1)}, u32[]{:S(2)}, u32[]{:S(2)}) %collective-permute-start.12) | collective-permute-done | bytes 345632 | tf_op jit(solution)/shard_map/ppermute | solution.py:40
  107.6 8.4 %collective-permute-start.7 = (f32[2,448]{1,0:T(2,128)S(1)}, f32[2,448]{1,0:T(2,128)S(1)}, u32[]{:S(2)}, u32[]{:S(2)}) collective-permute-start(f32[2,448]{1,0:T(2,128)S(1)} %fusion.153), channel_id=1, source_target_pairs={{0,2},{1,3},{2,0},{3,1},{4,6},{5,7},{6,4},{7,5},{8,10},{9,11},{10,... | collective-permute-start | bytes 10760 | tf_op jit(solution)/shard_map/ppermute | solution.py:40
  117.6 3.4 collective-permute-start.19
  125.1 4.6 collective-permute-start.9
  134.6 4.2 collective-permute-done.10
  142.0 9.8 %reshape.985 = bf16[320,27,160]{2,1,0:T(8,128)(2,1)} reshape(bf16[4,80,4320]{2,1,0:T(8,128)(2,1)} %pad_maximum_fusion) | data formatting | bytes 5529600 | tf_op jit(solution)/shard_map/reshape;reshape | solution.py:157
  151.9 8.1 %copy.719 = bf16[320,27,160]{0,2,1:T(8,128)(2,1)} copy(bf16[320,27,160]{2,1,0:T(8,128)(2,1)} %reshape.985) | data formatting | bytes 5529600 | tf_op jit(solution)/shard_map/reshape;reshape | solution.py:157
  160.0 2.9 pad_add_fusion
  162.9 6.0 %fusion.12 = f32[8,2,8,8,448]{4,0,3,2,1:T(8,128)S(1)} fusion(bf16[3,3,3,192,448]{4,3,2,1,0:T(8,128)(2,1)S(1)} %bitcast.221, bf16[8,4,8,8,192]{4,3,2,1,0:T(8,128)(2,1)S(1)} %copy-done.27), kind=kOutput, calls=%fused_computation.64 | convolution fusion | flops 3996647424 | bytes 7266304 | tf_op jit(solution)/shard_map/conv_general_dilated | solution.py:101
  173.8 3.3 reshape_reshape.16
  203.4 4.2 copy.664
  220.3 4.5 collective-permute-start.38
  227.5 2.7 collective-permute-start.41
  238.6 3.3 collective-permute-done.35
  267.0 3.1 convolution_convert_fusion.2
  280.5 3.7 copy.734
  284.2 3.4 convert_element_type.517
  312.1 4.7 collective-permute-start.64
  324.6 3.0 collective-permute-done.57
  339.6 3.4 broadcast_in_dim.42
  358.1 3.5 multiply_convert_fusion
  362.8 3.9 fusion.4
  369.1 7.7 %fusion.17 = f32[8,2,8,8,192]{4,0,3,2,1:T(8,128)S(1)} fusion(bf16[3,3,3,448,192]{3,4,2,1,0:T(8,128)(2,1)S(1)} %bitcast.226, bf16[8,2,8,8,448]{4,3,2,1,0:T(8,128)(2,1)S(1)} %slice.759), kind=kOutput, calls=%fused_computation.82 | convolution fusion | flops 2664431616 | bytes 6348800 | tf_op jit(solution)/shard_map/conv_general_dilated | solution.py:101
  376.7 10.7 %convolution_convert_fusion = bf16[3,3,3,192,448]{4,3,2,1,0:T(8,128)(2,1)S(1)} fusion(bf16[8,4,8,8,192]{4,3,2,1,0:T(8,128)(2,1)S(1)} %copy-done.28, bf16[8,2,8,8,448]{4,3,2,1,0:T(8,128)(2,1)S(1)} %slice.759), kind=kOutput, calls=%fused_computation.3 | convolution fusion | flops 3998969856 | bytes 6348800 | tf_op jit(solution)/shard_map/conv_general_dilated | solution.py:107
  390.3 4.6 collective-permute-start.78
  398.1 9.1 %convert_element_type.472 = bf16[4,80,4320]{1,0,2:T(4,128)(2,1)} reshape(bf16[320,27,160]{0,2,1:T(8,128)(2,1)} %slice_bitcast_fusion) | data formatting | bytes 5529600 | tf_op jit(solution)/shard_map/convert_element_type | solution.py:178
  407.2 11.1 %constant_dynamic-slice_fusion.10 = (bf16[4,40,4320]{1,0,2:T(4,128)(2,1)}, bf16[4,40,4320]{1,0,2:T(4,128)(2,1)}) fusion(bf16[4,80,4320]{1,0,2:T(4,128)(2,1)} %convert_element_type.472, s32[]{:T(128)S(6)} %select_n.1130, s32[]{:T(128)S(6)} %select_n.1131), kind=kLoop, calls=%fused_computation.380 | loop fusion | bytes 5529608 | tf_op jit(solution)/shard_map/dynamic_slice | solution.py:184
  427.5 6.5 %copy.732 = bf16[4,40,4320]{2,1,0:T(8,128)(2,1)} copy(bf16[4,40,4320]{1,0,2:T(4,128)(2,1)} %get-tuple-element.225) | data formatting | bytes 2764800
  434.0 6.5 %copy.690 = bf16[4,40,4320]{2,1,0:T(8,128)(2,1)} copy(bf16[4,40,4320]{1,0,2:T(4,128)(2,1)} %get-tuple-element.226) | data formatting | bytes 2764800 | tf_op jit(solution)/shard_map/dynamic_slice | solution.py:185
  444.7 5.4 collective-permute-start.71
  477.2 2.9 fusion.37
  491.2 4.2 collective-permute-done.114
  506.1 7.4 %collective-permute-done.81 = bf16[4,36,528]{2,1,0:T(8,128)(2,1)S(1)} collective-permute-done((bf16[4,36,528]{2,1,0:T(8,128)(2,1)S(1)}, bf16[4,36,528]{2,1,0:T(8,128)(2,1)S(1)}, u32[]{:S(2)}, u32[]{:S(2)}) %collective-permute-start.81) | collective-permute-done | bytes 152096 | tf_op jit(solution)/shard_map/ppermute | solution.py:189
  522.4 3.0 collective-permute-start.108
  527.9 3.6 collective-permute-done.109
  540.5 4.2 collective-permute-done.90
  545.0 5.2 collective-permute-done.91
  552.7 3.6 collective-permute-done.93
  561.4 4.0 collective-permute-done.94
  571.6 3.2 fusion.7
  574.7 6.4 %reshape.979 = f32[2,345600]{1,0:T(2,128)} reshape(f32[2,80,4320]{2,1,0:T(8,128)} %fusion.7) | data formatting | bytes 5529600 | tf_op jit(solution)/shard_map/convert_element_type | solution.py:204
  581.1 3.1 fusion.6
  584.3 6.6 %reshape.974 = f32[2,345600]{1,0:T(2,128)} reshape(f32[2,80,4320]{2,1,0:T(8,128)} %fusion.6) | data formatting | bytes 5529600 | tf_op jit(solution)/shard_map/convert_element_type | solution.py:204
  (802 shorter events, 325.6 us)
Async XLA Ops:
  3.9 47.4 %collective-permute-start.17 = (bf16[16,864]{1,0:T(8,128)(2,1)}, bf16[16,864]{1,0:T(8,128)(2,1)}, u32[]{:S(2)}, u32[]{:S(2)}) collective-permute-start(bf16[16,864]{1,0:T(8,128)(2,1)} %constant_dynamic-slice_fusion.14), channel_id=1, source_target_pairs={{0,1},{1,0},{2,3},{3,2},{4,5},{5,4},{6,7},{7,6},{8,9},{9,8},{10,11... | collective-permute-start | bytes 82952 | tf_op jit(solution)/shard_map/ppermute | solution.py:40
  6.9 44.4 %collective-permute-start.16 = (bf16[16,864]{1,0:T(8,128)(2,1)}, bf16[16,864]{1,0:T(8,128)(2,1)}, u32[]{:S(2)}, u32[]{:S(2)}) collective-permute-start(bf16[16,864]{1,0:T(8,128)(2,1)} %constant_dynamic-slice_fusion.14), channel_id=1, source_target_pairs={{0,2},{1,3},{2,0},{3,1},{4,6},{5,7},{6,4},{7,5},{8,10},{9,11},{10,... | collective-permute-start | bytes 82952 | tf_op jit(solution)/shard_map/ppermute | solution.py:40
  9.5 42.4 %collective-permute-start.15 = (bf16[16,864]{1,0:T(8,128)(2,1)}, bf16[16,864]{1,0:T(8,128)(2,1)}, u32[]{:S(2)}, u32[]{:S(2)}) collective-permute-start(bf16[16,864]{1,0:T(8,128)(2,1)} %constant_dynamic-slice_fusion.14), channel_id=1, source_target_pairs={{0,3},{1,2},{2,1},{3,0},{4,7},{5,6},{6,5},{7,4},{8,11},{9,10},{10,... | collective-permute-start | bytes 82952 | tf_op jit(solution)/shard_map/ppermute | solution.py:40
  13.5 43.1 %collective-permute-start.2 = (bf16[80,528]{1,0:T(8,128)(2,1)S(1)}, bf16[80,528]{1,0:T(8,128)(2,1)}, u32[]{:S(2)}, u32[]{:S(2)}) collective-permute-start(bf16[80,528]{1,0:T(8,128)(2,1)S(1)} %fusion.60), channel_id=1, source_target_pairs={{0,1},{1,0},{2,3},{3,2},{4,5},{5,4},{6,7},{7,6},{8,9},{9,8},{10,11... | collective-permute-start | bytes 253448 | tf_op jit(solution)/shard_map/ppermute | solution.py:40
  14.5 42.3 %collective-permute-start.1 = (bf16[80,528]{1,0:T(8,128)(2,1)S(1)}, bf16[80,528]{1,0:T(8,128)(2,1)}, u32[]{:S(2)}, u32[]{:S(2)}) collective-permute-start(bf16[80,528]{1,0:T(8,128)(2,1)S(1)} %fusion.60), channel_id=1, source_target_pairs={{0,2},{1,3},{2,0},{3,1},{4,6},{5,7},{6,4},{7,5},{8,10},{9,11},{10,... | collective-permute-start | bytes 253448 | tf_op jit(solution)/shard_map/ppermute | solution.py:40
  51.4 11.6 %collective-permute-start.28 = (bf16[80,832]{1,0:T(8,128)(2,1)S(1)}, bf16[80,832]{1,0:T(8,128)(2,1)S(1)}, u32[]{:S(2)}, u32[]{:S(2)}) collective-permute-start(bf16[80,832]{1,0:T(8,128)(2,1)S(1)} %fusion.53), channel_id=1, source_target_pairs={{0,1},{1,0},{2,3},{3,2},{4,5},{5,4},{6,7},{7,6},{8,9},{9,8},{10,11... | collective-permute-start | bytes 399368 | tf_op jit(solution)/shard_map/ppermute | solution.py:40
  51.9 15.4 %collective-permute-start.27 = (bf16[80,832]{1,0:T(8,128)(2,1)S(1)}, bf16[80,832]{1,0:T(8,128)(2,1)S(1)}, u32[]{:S(2)}, u32[]{:S(2)}) collective-permute-start(bf16[80,832]{1,0:T(8,128)(2,1)S(1)} %fusion.53), channel_id=1, source_target_pairs={{0,2},{1,3},{2,0},{3,1},{4,6},{5,7},{6,4},{7,5},{8,10},{9,11},{10,... | collective-permute-start | bytes 399368 | tf_op jit(solution)/shard_map/ppermute | solution.py:40
  56.6 11.6 %collective-permute-start.26 = (bf16[80,832]{1,0:T(8,128)(2,1)S(1)}, bf16[80,832]{1,0:T(8,128)(2,1)S(1)}, u32[]{:S(2)}, u32[]{:S(2)}) collective-permute-start(bf16[80,832]{1,0:T(8,128)(2,1)S(1)} %fusion.53), channel_id=1, source_target_pairs={{0,3},{1,2},{2,1},{3,0},{4,7},{5,6},{6,5},{7,4},{8,11},{9,10},{10,... | collective-permute-start | bytes 399368 | tf_op jit(solution)/shard_map/ppermute | solution.py:40
  56.7 19.1 %collective-permute-start.13 = (bf16[40,4320]{1,0:T(8,128)(2,1)}, bf16[40,4320]{1,0:T(8,128)(2,1)}, u32[]{:S(2)}, u32[]{:S(2)}) collective-permute-start(bf16[40,4320]{1,0:T(8,128)(2,1)} %constant_dynamic-slice_fusion.15), channel_id=1, source_target_pairs={{0,1},{1,0},{2,3},{3,2},{4,5},{5,4},{6,7},{7,6},{8,9},{9,8},{10,11... | collective-permute-start | bytes 1036808 | tf_op jit(solution)/shard_map/ppermute | solution.py:40
  59.1 35.0 %collective-permute-start.12 = (bf16[40,4320]{1,0:T(8,128)(2,1)}, bf16[40,4320]{1,0:T(8,128)(2,1)}, u32[]{:S(2)}, u32[]{:S(2)}) collective-permute-start(bf16[40,4320]{1,0:T(8,128)(2,1)} %constant_dynamic-slice_fusion.15), channel_id=1, source_target_pairs={{0,2},{1,3},{2,0},{3,1},{4,6},{5,7},{6,4},{7,5},{8,10},{9,11},{10,... | collective-permute-start | bytes 1036808 | tf_op jit(solution)/shard_map/ppermute | solution.py:40
  63.0 31.1 %collective-permute-start.11 = (bf16[40,4320]{1,0:T(8,128)(2,1)}, bf16[40,4320]{1,0:T(8,128)(2,1)}, u32[]{:S(2)}, u32[]{:S(2)}) collective-permute-start(bf16[40,4320]{1,0:T(8,128)(2,1)} %constant_dynamic-slice_fusion.15), channel_id=1, source_target_pairs={{0,3},{1,2},{2,1},{3,0},{4,7},{5,6},{6,5},{7,4},{8,11},{9,10},{10,... | collective-permute-start | bytes 1036808 | tf_op jit(solution)/shard_map/ppermute | solution.py:40
  67.3 142.7 %collective-permute-start.48 = (bf16[8,1,4,4,112]{4,0,3,2,1:T(8,128)(2,1)}, bf16[8,1,4,4,112]{4,0,3,2,1:T(8,128)(2,1)}, u32[]{:S(2)}, u32[]{:S(2)}) collective-permute-start(bf16[8,1,4,4,112]{4,0,3,2,1:T(8,128)(2,1)} %get-tuple-element.214), channel_id=1, source_target_pairs={{0,3},{1,2},{2,1},{3,0},{4,7},{5,6},{6,5},{7,4},{8,11},{9,10},{10,... | collective-permute-start | bytes 86024 | tf_op jit(solution)/shard_map/ppermute | solution.py:59
  69.5 140.5 %collective-permute-start.50 = (bf16[8,1,4,4,112]{4,0,3,2,1:T(8,128)(2,1)}, bf16[8,1,4,4,112]{4,0,3,2,1:T(8,128)(2,1)}, u32[]{:S(2)}, u32[]{:S(2)}) collective-permute-start(bf16[8,1,4,4,112]{4,0,3,2,1:T(8,128)(2,1)} %get-tuple-element.290), channel_id=1, source_target_pairs={{0,1},{1,0},{2,3},{3,2},{4,5},{5,4},{6,7},{7,6},{8,9},{9,8},{10,11... | collective-permute-start | bytes 86024 | tf_op jit(solution)/shard_map/ppermute | solution.py:59
  75.9 19.7 %collective-permute-start.3 = (bf16[4,80,528]{2,1,0:T(8,128)(2,1)}, bf16[4,80,528]{2,1,0:T(8,128)(2,1)S(1)}, u32[]{:S(2)}, u32[]{:S(2)}) collective-permute-start(bf16[4,80,528]{2,1,0:T(8,128)(2,1)} %pad_maximum_fusion.10), channel_id=1, source_target_pairs={{0,4},{4,0},{8,12},{12,8},{16,20},{20,16},{24,28},{28,24},{1,5},{5... | collective-permute-start | bytes 1013768 | tf_op jit(solution)/shard_map/ppermute | solution.py:85
  116.3 23.7 %collective-permute-start.14 = (bf16[4,40,4320]{2,1,0:T(8,128)(2,1)S(1)}, bf16[4,40,4320]{2,1,0:T(8,128)(2,1)S(1)}, u32[]{:S(2)}, u32[]{:S(2)}) collective-permute-start(bf16[4,40,4320]{2,1,0:T(8,128)(2,1)S(1)} %pad_maximum_fusion.2), channel_id=1, source_target_pairs={{0,4},{4,0},{8,12},{12,8},{16,20},{20,16},{24,28},{28,24},{1,5},{5... | collective-permute-start | bytes 4147208 | tf_op jit(solution)/shard_map/ppermute | solution.py:85
  134.5 47.0 %collective-permute-start.29 = (bf16[4,80,832]{2,1,0:T(8,128)(2,1)}, bf16[4,80,832]{2,1,0:T(8,128)(2,1)}, u32[]{:S(2)}, u32[]{:S(2)}) collective-permute-start(bf16[4,80,832]{2,1,0:T(8,128)(2,1)} %pad_maximum_fusion.7), channel_id=1, source_target_pairs={{0,4},{4,0},{8,12},{12,8},{16,20},{20,16},{24,28},{28,24},{1,5},{5... | collective-permute-start | bytes 1597448 | tf_op jit(solution)/shard_map/ppermute | solution.py:85
  190.6 19.4 %collective-permute-start.49 = (bf16[8,1,4,4,112]{4,0,3,2,1:T(8,128)(2,1)}, bf16[8,1,4,4,112]{4,0,3,2,1:T(8,128)(2,1)}, u32[]{:S(2)}, u32[]{:S(2)}) collective-permute-start(bf16[8,1,4,4,112]{4,0,3,2,1:T(8,128)(2,1)} %get-tuple-element.291), channel_id=1, source_target_pairs={{0,2},{1,3},{2,0},{3,1},{4,6},{5,7},{6,4},{7,5},{8,10},{9,11},{10,... | collective-permute-start | bytes 86024 | tf_op jit(solution)/shard_map/ppermute | solution.py:59
  212.8 12.0 %collective-permute-start.34 = (f32[2,448]{1,0:T(2,128)S(1)}, f32[2,448]{1,0:T(2,128)S(1)}, u32[]{:S(2)}, u32[]{:S(2)}) collective-permute-start(f32[2,448]{1,0:T(2,128)S(1)} %fusion.151), channel_id=1, source_target_pairs={{0,3},{1,2},{2,1},{3,0},{4,7},{5,6},{6,5},{7,4},{8,11},{9,10},{10,... | collective-permute-start | bytes 10760 | tf_op jit(solution)/shard_map/ppermute | solution.py:40
  258.4 40.3 %collective-permute-start.46 = (bf16[8,1,4,4,112]{4,0,3,2,1:T(8,128)(2,1)}, bf16[8,1,4,4,112]{4,0,3,2,1:T(8,128)(2,1)}, u32[]{:S(2)}, u32[]{:S(2)}) collective-permute-start(bf16[8,1,4,4,112]{4,0,3,2,1:T(8,128)(2,1)} %get-tuple-element.219), channel_id=1, source_target_pairs={{0,2},{1,3},{2,0},{3,1},{4,6},{5,7},{6,4},{7,5},{8,10},{9,11},{10,... | collective-permute-start | bytes 86024 | tf_op jit(solution)/shard_map/ppermute | solution.py:59
  258.9 41.5 %collective-permute-start.47 = (bf16[8,1,4,4,112]{4,0,3,2,1:T(8,128)(2,1)}, bf16[8,1,4,4,112]{4,0,3,2,1:T(8,128)(2,1)}, u32[]{:S(2)}, u32[]{:S(2)}) collective-permute-start(bf16[8,1,4,4,112]{4,0,3,2,1:T(8,128)(2,1)} %get-tuple-element.292), channel_id=1, source_target_pairs={{0,1},{1,0},{2,3},{3,2},{4,5},{5,4},{6,7},{7,6},{8,9},{9,8},{10,11... | collective-permute-start | bytes 86024 | tf_op jit(solution)/shard_map/ppermute | solution.py:59
  262.4 29.5 %collective-permute-start.62 = (f32[2,128]{1,0:T(2,128)}, f32[2,128]{1,0:T(2,128)}, u32[]{:S(2)}, u32[]{:S(2)}) collective-permute-start(f32[2,128]{1,0:T(2,128)} %slice.751), channel_id=1, source_target_pairs={{0,2},{1,3},{2,0},{3,1},{4,6},{5,7},{6,4},{7,5},{8,10},{9,11},{10,... | collective-permute-start | bytes 3080 | tf_op jit(solution)/shard_map/ppermute | solution.py:40
  263.0 30.8 %collective-permute-start.63 = (f32[2,128]{1,0:T(2,128)}, f32[2,128]{1,0:T(2,128)}, u32[]{:S(2)}, u32[]{:S(2)}) collective-permute-start(f32[2,128]{1,0:T(2,128)} %slice.751), channel_id=1, source_target_pairs={{0,3},{1,2},{2,1},{3,0},{4,7},{5,6},{6,5},{7,4},{8,11},{9,10},{10,... | collective-permute-start | bytes 3080 | tf_op jit(solution)/shard_map/ppermute | solution.py:40
  264.8 29.2 %collective-permute-start.61 = (f32[2,128]{1,0:T(2,128)}, f32[2,128]{1,0:T(2,128)}, u32[]{:S(2)}, u32[]{:S(2)}) collective-permute-start(f32[2,128]{1,0:T(2,128)} %slice.751), channel_id=1, source_target_pairs={{0,1},{1,0},{2,3},{3,2},{4,5},{5,4},{6,7},{7,6},{8,9},{9,8},{10,11... | collective-permute-start | bytes 3080 | tf_op jit(solution)/shard_map/ppermute | solution.py:40
  293.7 26.2 %collective-permute-start.53 = (bf16[8,1,4,4,192]{4,0,3,2,1:T(8,128)(2,1)}, bf16[8,1,4,4,192]{4,0,3,2,1:T(8,128)(2,1)}, u32[]{:S(2)}, u32[]{:S(2)}) collective-permute-start(bf16[8,1,4,4,192]{4,0,3,2,1:T(8,128)(2,1)} %get-tuple-element.262), channel_id=1, source_target_pairs={{0,1},{1,0},{2,3},{3,2},{4,5},{5,4},{6,7},{7,6},{8,9},{9,8},{10,11... | collective-permute-start | bytes 147464 | tf_op jit(solution)/shard_map/ppermute | solution.py:59
  294.0 26.0 %collective-permute-start.54 = (bf16[8,1,4,4,192]{4,0,3,2,1:T(8,128)(2,1)}, bf16[8,1,4,4,192]{4,0,3,2,1:T(8,128)(2,1)}, u32[]{:S(2)}, u32[]{:S(2)}) collective-permute-start(bf16[8,1,4,4,192]{4,0,3,2,1:T(8,128)(2,1)} %get-tuple-element.263), channel_id=1, source_target_pairs={{0,2},{1,3},{2,0},{3,1},{4,6},{5,7},{6,4},{7,5},{8,10},{9,11},{10,... | collective-permute-start | bytes 147464 | tf_op jit(solution)/shard_map/ppermute | solution.py:59
  298.7 21.3 %collective-permute-start.55 = (bf16[8,1,4,4,192]{4,0,3,2,1:T(8,128)(2,1)}, bf16[8,1,4,4,192]{4,0,3,2,1:T(8,128)(2,1)}, u32[]{:S(2)}, u32[]{:S(2)}) collective-permute-start(bf16[8,1,4,4,192]{4,0,3,2,1:T(8,128)(2,1)} %get-tuple-element.264), channel_id=1, source_target_pairs={{0,3},{1,2},{2,1},{3,0},{4,7},{5,6},{6,5},{7,4},{8,11},{9,10},{10,... | collective-permute-start | bytes 147464 | tf_op jit(solution)/shard_map/ppermute | solution.py:59
  300.5 11.7 %collective-permute-start.118 = (bf16[16,864]{1,0:T(8,128)(2,1)}, bf16[16,864]{1,0:T(8,128)(2,1)}, u32[]{:S(2)}, u32[]{:S(2)}) collective-permute-start(bf16[16,864]{1,0:T(8,128)(2,1)} %constant_dynamic-slice_fusion.1), channel_id=1, source_target_pairs={{0,4},{4,0},{8,12},{12,8},{16,20},{20,16},{24,28},{28,24},{1,5},{5... | collective-permute-start | bytes 82952 | tf_op jit(solution)/shard_map/ppermute | solution.py:189
  300.5 17.2 %collective-permute-start.65 = (bf16[8,1,4,4,128]{4,0,3,2,1:T(8,128)(2,1)}, bf16[8,1,4,4,128]{4,0,3,2,1:T(8,128)(2,1)}, u32[]{:S(2)}, u32[]{:S(2)}) collective-permute-start(bf16[8,1,4,4,128]{4,0,3,2,1:T(8,128)(2,1)} %get-tuple-element.298), channel_id=1, source_target_pairs={{1,0},{2,1},{3,2},{5,4},{6,5},{7,6},{9,8},{10,9},{11,10},{13,12},{... | collective-permute-start | bytes 98312 | tf_op jit(solution)/shard_map/ppermute | solution.py:96
  317.7 168.5 %collective-permute-start.113 = (bf16[40,4320]{1,0:T(8,128)(2,1)}, bf16[40,4320]{1,0:T(8,128)(2,1)}, u32[]{:S(2)}, u32[]{:S(2)}) collective-permute-start(bf16[40,4320]{1,0:T(8,128)(2,1)} %constant_dynamic-slice_fusion.3), channel_id=1, source_target_pairs={{0,4},{4,0},{8,12},{12,8},{16,20},{20,16},{24,28},{28,24},{1,5},{5... | collective-permute-start | bytes 1036808 | tf_op jit(solution)/shard_map/ppermute | solution.py:189
  332.0 21.6 %collective-permute-start.121 = (bf16[2,8,864]{2,1,0:T(8,128)(2,1)S(1)}, bf16[2,8,864]{2,1,0:T(8,128)(2,1)S(1)}, u32[]{:S(2)}, u32[]{:S(2)}) collective-permute-start(bf16[2,8,864]{2,1,0:T(8,128)(2,1)S(1)} %maximum_select_fusion.15), channel_id=1, source_target_pairs={{0,8},{4,12},{8,0},{12,4},{16,24},{20,28},{24,16},{28,20},{1,9},{5... | collective-permute-start | bytes 82952 | tf_op jit(solution)/shard_map/ppermute | solution.py:199
  349.1 148.8 %collective-permute-start.105 = (bf16[4,72,832]{2,1,0:T(8,128)(2,1)}, bf16[4,72,832]{2,1,0:T(8,128)(2,1)}, u32[]{:S(2)}, u32[]{:S(2)}) collective-permute-start(bf16[4,72,832]{2,1,0:T(8,128)(2,1)} %fusion.34), channel_id=1, source_target_pairs={{0,4},{4,0},{8,12},{12,8},{16,20},{20,16},{24,28},{28,24},{1,5},{5... | collective-permute-start | bytes 1437704 | tf_op jit(solution)/shard_map/ppermute | solution.py:189
  357.3 83.2 %collective-permute-start.122 = (bf16[2,16,864]{2,1,0:T(8,128)(2,1)S(1)}, bf16[2,16,864]{2,1,0:T(8,128)(2,1)}, u32[]{:S(2)}, u32[]{:S(2)}) collective-permute-start(bf16[2,16,864]{2,1,0:T(8,128)(2,1)S(1)} %maximum_select_fusion.13), channel_id=1, source_target_pairs={{0,4},{4,0},{8,12},{12,8},{16,20},{20,16},{24,28},{28,24},{1,5},{5... | collective-permute-start | bytes 165896 | tf_op jit(solution)/shard_map/ppermute | solution.py:199
  390.3 54.3 %collective-permute-start.78 = (bf16[8,1,8,8,128]{4,3,2,1,0:T(8,128)(2,1)}, bf16[8,1,8,8,128]{4,3,2,1,0:T(8,128)(2,1)}, u32[]{:S(2)}, u32[]{:S(2)}) collective-permute-start(bf16[8,1,8,8,128]{4,3,2,1,0:T(8,128)(2,1)} %get-tuple-element.233), channel_id=1, source_target_pairs={{0,1},{1,2},{2,3},{4,5},{5,6},{6,7},{8,9},{9,10},{10,11},{12,13},{... | collective-permute-start | bytes 393224 | tf_op jit(solution)/shard_map/ppermute | solution.py:95
  394.9 55.2 %collective-permute-start.79 = (bf16[8,1,8,8,128]{4,3,2,1,0:T(8,128)(2,1)}, bf16[8,1,8,8,128]{4,3,2,1,0:T(8,128)(2,1)}, u32[]{:S(2)}, u32[]{:S(2)}) collective-permute-start(bf16[8,1,8,8,128]{4,3,2,1,0:T(8,128)(2,1)} %get-tuple-element.234), channel_id=1, source_target_pairs={{1,0},{2,1},{3,2},{5,4},{6,5},{7,6},{9,8},{10,9},{11,10},{13,12},{... | collective-permute-start | bytes 393224 | tf_op jit(solution)/shard_map/ppermute | solution.py:96
  442.4 13.8 %collective-permute-start.72 = (bf16[8,1,8,8,192]{4,3,2,1,0:T(8,128)(2,1)S(1)}, bf16[8,1,8,8,192]{4,3,2,1,0:T(8,128)(2,1)S(1)}, u32[]{:S(2)}, u32[]{:S(2)}) collective-permute-start(bf16[8,1,8,8,192]{4,3,2,1,0:T(8,128)(2,1)S(1)} %copy.763), channel_id=1, source_target_pairs={{1,0},{2,1},{3,2},{5,4},{6,5},{7,6},{9,8},{10,9},{11,10},{13,12},{... | collective-permute-start | bytes 589832 | tf_op jit(solution)/shard_map/ppermute | solution.py:368
  444.7 11.4 %collective-permute-start.71 = (bf16[8,1,8,8,192]{4,3,2,1,0:T(8,128)(2,1)S(1)}, bf16[8,1,8,8,192]{4,3,2,1,0:T(8,128)(2,1)S(1)}, u32[]{:S(2)}, u32[]{:S(2)}) collective-permute-start(bf16[8,1,8,8,192]{4,3,2,1,0:T(8,128)(2,1)S(1)} %copy-done.57), channel_id=1, source_target_pairs={{0,1},{1,2},{2,3},{4,5},{5,6},{6,7},{8,9},{9,10},{10,11},{12,13},{... | collective-permute-start | bytes 589832 | tf_op jit(solution)/shard_map/ppermute | solution.py:369
  473.8 44.5 %collective-permute-start.88 = (bf16[4,40,4320]{2,1,0:T(8,128)(2,1)}, bf16[4,40,4320]{2,1,0:T(8,128)(2,1)}, u32[]{:S(2)}, u32[]{:S(2)}) collective-permute-start(bf16[4,40,4320]{2,1,0:T(8,128)(2,1)} %copy.690), channel_id=1, source_target_pairs={{0,4},{4,0},{8,12},{12,8},{16,20},{20,16},{24,28},{28,24},{1,5},{5... | collective-permute-start | bytes 4147208 | tf_op jit(solution)/shard_map/ppermute | solution.py:189
  483.9 16.7 %collective-permute-start.80 = (bf16[4,72,528]{2,1,0:T(8,128)(2,1)}, bf16[4,72,528]{2,1,0:T(8,128)(2,1)}, u32[]{:S(2)}, u32[]{:S(2)}) collective-permute-start(bf16[4,72,528]{2,1,0:T(8,128)(2,1)} %fusion.41), channel_id=1, source_target_pairs={{0,4},{4,0},{8,12},{12,8},{16,20},{20,16},{24,28},{28,24},{1,5},{5... | collective-permute-start | bytes 912392 | tf_op jit(solution)/shard_map/ppermute | solution.py:189
  499.3 17.6 %collective-permute-start.106 = (bf16[4,36,832]{2,1,0:T(8,128)(2,1)S(1)}, bf16[4,36,832]{2,1,0:T(8,128)(2,1)S(1)}, u32[]{:S(2)}, u32[]{:S(2)}) collective-permute-start(bf16[4,36,832]{2,1,0:T(8,128)(2,1)S(1)} %constant_dynamic-slice_fusion.4), channel_id=1, source_target_pairs={{0,8},{4,12},{8,0},{12,4},{16,24},{20,28},{24,16},{28,20},{1,9},{5... | collective-permute-start | bytes 718856 | tf_op jit(solution)/shard_map/ppermute | solution.py:189
  501.8 11.7 %collective-permute-start.81 = (bf16[4,36,528]{2,1,0:T(8,128)(2,1)S(1)}, bf16[4,36,528]{2,1,0:T(8,128)(2,1)S(1)}, u32[]{:S(2)}, u32[]{:S(2)}) collective-permute-start(bf16[4,36,528]{2,1,0:T(8,128)(2,1)S(1)} %constant_dynamic-slice_fusion.11), channel_id=1, source_target_pairs={{0,8},{4,12},{8,0},{12,4},{16,24},{20,28},{24,16},{28,20},{1,9},{5... | collective-permute-start | bytes 456200 | tf_op jit(solution)/shard_map/ppermute | solution.py:189
  504.7 47.7 %collective-permute-start.116 = (bf16[2,20,4320]{2,0,1:T(2,128)(2,1)S(1)}, bf16[2,20,4320]{2,0,1:T(2,128)(2,1)S(1)}, u32[]{:S(2)}, u32[]{:S(2)}) collective-permute-start(bf16[2,20,4320]{2,0,1:T(2,128)(2,1)S(1)} %broadcast_select_fusion.2), channel_id=1, source_target_pairs={{0,8},{4,12},{8,0},{12,4},{16,24},{20,28},{24,16},{28,20},{1,9},{5... | collective-permute-start | bytes 1036808 | tf_op jit(solution)/shard_map/ppermute | solution.py:199
  520.9 13.2 %collective-permute-start.89 = (bf16[4,20,4320]{2,0,1:T(4,128)(2,1)S(1)}, bf16[4,20,4320]{2,0,1:T(4,128)(2,1)S(1)}, u32[]{:S(2)}, u32[]{:S(2)}) collective-permute-start(bf16[4,20,4320]{2,0,1:T(4,128)(2,1)S(1)} %copy.691), channel_id=1, source_target_pairs={{0,8},{4,12},{8,0},{12,4},{16,24},{20,28},{24,16},{28,20},{1,9},{5... | collective-permute-start | bytes 2073608 | tf_op jit(solution)/shard_map/ppermute | solution.py:189
  536.1 14.1 %collective-permute-start.91 = (bf16[20,4320]{1,0:T(8,128)(2,1)S(1)}, bf16[20,4320]{1,0:T(8,128)(2,1)S(1)}, u32[]{:S(2)}, u32[]{:S(2)}) collective-permute-start(bf16[20,4320]{1,0:T(8,128)(2,1)S(1)} %get-tuple-element.242), channel_id=1, source_target_pairs={{0,2},{1,3},{2,0},{3,1},{4,6},{5,7},{6,4},{7,5},{8,10},{9,11},{10,... | collective-permute-start | bytes 518408 | tf_op jit(solution)/shard_map/ppermute | solution.py:59
  537.5 12.7 %collective-permute-start.92 = (bf16[20,4320]{1,0:T(8,128)(2,1)S(1)}, bf16[20,4320]{1,0:T(8,128)(2,1)S(1)}, u32[]{:S(2)}, u32[]{:S(2)}) collective-permute-start(bf16[20,4320]{1,0:T(8,128)(2,1)S(1)} %get-tuple-element.243), channel_id=1, source_target_pairs={{0,3},{1,2},{2,1},{3,0},{4,7},{5,6},{6,5},{7,4},{8,11},{9,10},{10,... | collective-permute-start | bytes 518408 | tf_op jit(solution)/shard_map/ppermute | solution.py:59
  539.0 11.9 %collective-permute-start.86 = (bf16[2,36,528]{2,1,0:T(8,128)(2,1)S(1)}, bf16[2,36,528]{2,1,0:T(8,128)(2,1)S(1)}, u32[]{:S(2)}, u32[]{:S(2)}) collective-permute-start(bf16[2,36,528]{2,1,0:T(8,128)(2,1)S(1)} %maximum_select_fusion.11), channel_id=1, source_target_pairs={{0,8},{4,12},{8,0},{12,4},{16,24},{20,28},{24,16},{28,20},{1,9},{5... | collective-permute-start | bytes 228104 | tf_op jit(solution)/shard_map/ppermute | solution.py:199
  551.8 14.0 %collective-permute-start.112 = (bf16[2,72,832]{2,1,0:T(8,128)(2,1)}, bf16[2,72,832]{2,1,0:T(8,128)(2,1)}, u32[]{:S(2)}, u32[]{:S(2)}) collective-permute-start(bf16[2,72,832]{2,1,0:T(8,128)(2,1)} %maximum_select_fusion.6), channel_id=1, source_target_pairs={{0,4},{4,0},{8,12},{12,8},{16,20},{20,16},{24,28},{28,24},{1,5},{5... | collective-permute-start | bytes 718856 | tf_op jit(solution)/shard_map/ppermute | solution.py:199
  558.8 12.7 %collective-permute-start.117 = (bf16[2,40,4320]{2,1,0:T(8,128)(2,1)S(1)}, bf16[2,40,4320]{2,1,0:T(8,128)(2,1)}, u32[]{:S(2)}, u32[]{:S(2)}) collective-permute-start(bf16[2,40,4320]{2,1,0:T(8,128)(2,1)S(1)} %maximum_select_fusion.3), channel_id=1, source_target_pairs={{0,4},{4,0},{8,12},{12,8},{16,20},{20,16},{24,28},{28,24},{1,5},{5... | collective-permute-start | bytes 2073608 | tf_op jit(solution)/shard_map/ppermute | solution.py:199
  565.8 15.4 %collective-permute-start.95 = (bf16[2,40,4320]{2,1,0:T(8,128)(2,1)S(1)}, bf16[2,40,4320]{2,1,0:T(8,128)(2,1)}, u32[]{:S(2)}, u32[]{:S(2)}) collective-permute-start(bf16[2,40,4320]{2,1,0:T(8,128)(2,1)S(1)} %maximum_select_fusion.2), channel_id=1, source_target_pairs={{0,4},{4,0},{8,12},{12,8},{16,20},{20,16},{24,28},{28,24},{1,5},{5... | collective-permute-start | bytes 2073608 | tf_op jit(solution)/shard_map/ppermute | solution.py:199
  (213 other events, 1952.6 us)
